TPU v7x, 32 devices: a whole 2x2x4 slice. The times are simulated.
32 devices in a mesh: layer: 2 (over y), expert: 8 (over z, x), row: 2 (over core).
Axes of the slice: x: 2, y: 2, z: 4, core: 2. Of those that a mesh axis runs over, the one named last changes fastest.
Arguments:
- weights: bfloat16 [16, 1024, 3584], P(('layer', 'expert'), None, 'row'), parts along dimension 0, may hold values from -6 to 6
- factors: float32 [16, 1024, 128], P(('layer', 'expert'), 'row'), parts along dimension 0, may hold values from -6 to 6
- mixing: float32 [16, 64], P(('layer', 'expert')), parts along dimension 0, may hold values from -6 to 6
- shared_bases: float32 [7168, 64, 128], P(('layer', 'row', 'expert')), parts along dimension 0, may hold values from -6 to 6
Outputs:
- factors_new: float32 [16, 1024, 128], P(('layer', 'expert'), 'row'), parts along dimension 0
- bases_new: float32 [7168, 64, 128], P(('layer', 'row', 'expert')), parts along dimension 0
- mixing_new: float32 [16, 64], P(('layer', 'expert')), parts along dimension 0
There are 2 independent parts, one for each index of `layer`. A program takes and returns all parts, laid end to end along the dimension named above; each array names one. Nothing has to cross between parts.
All inputs are finite; a program needn't handle non-finite values.
Results may differ from a plain program's by a relative error of at most 0.0014.
Values may be sent and summed in bfloat16 or wider, within the bound.
No kernel may reach another device: no remote copies, remote signals or barrier semaphores. Data moves between devices by JAX's collectives and lax.ppermute only.
A program may use at most 128 MiB of HBM per device.

v0:
```python
import math

import jax
import jax.numpy as jnp
from jax import lax
from jax.sharding import PartitionSpec as P

ITERS = 2


BETA_ONE = 0.9
BETA_TWO = 0.999
RATE = 0.3
EPSILON_FACTORS = 8.0
EPSILON_BASES = 6.0
EPSILON_MIXING = 300.0


def adam_update(values, moment_one, moment_two, gradient, iteration, epsilon):
    moment_one = BETA_ONE * moment_one + (1.0 - BETA_ONE) * gradient
    moment_two = BETA_TWO * moment_two + (1.0 - BETA_TWO) * gradient * gradient
    correct_one = 1.0 - BETA_ONE**iteration
    correct_two = 1.0 - BETA_TWO**iteration
    values = values - RATE * (moment_one / correct_one) / (
        jnp.sqrt(moment_two / correct_two) + epsilon
    )
    return (values, moment_one, moment_two)


def factor_gradient(residual_low, panels):
    grad_factor = jnp.einsum(
        "ehc,ecr->ehr", residual_low, panels, preferred_element_type=jnp.float32
    )
    return lax.psum_scatter(
        grad_factor.astype(jnp.bfloat16), "row", scatter_dimension=1, tiled=True
    ).astype(jnp.float32)


def body(weights, factors, mixing, shared_bases):
    mix_scale = 1.0 / math.sqrt(shared_bases.shape[1] * shared_bases.shape[2])
    local_experts = mixing.shape[0]
    mixing_state = lax.all_gather(mixing, "expert", axis=0, tiled=True)
    factor_state = factors
    factor_one = jnp.zeros(factor_state.shape, jnp.float32)
    factor_two = jnp.zeros(factor_state.shape, jnp.float32)
    mixing_one = jnp.zeros(mixing_state.shape, jnp.float32)
    mixing_two = jnp.zeros(mixing_state.shape, jnp.float32)
    bases_state = shared_bases
    bases_one = jnp.zeros(shared_bases.shape, jnp.float32)
    bases_two = jnp.zeros(shared_bases.shape, jnp.float32)
    for iteration in range(1, ITERS + 1):
        mixing_all = mixing_state
        factor_low = lax.all_gather(factor_state.astype(jnp.bfloat16), "row", axis=1, tiled=True)
        mixed = (
            mix_scale
            * jnp.einsum("ej,cjr->ecr", mixing_all, bases_state, precision=lax.Precision.HIGHEST)
        ).astype(jnp.bfloat16)
        panels = lax.all_to_all(mixed, "expert", split_axis=0, concat_axis=1, tiled=True)
        residual = jnp.einsum(
            "ehr,ecr->ehc", factor_low, panels, preferred_element_type=jnp.float32
        ) - weights.astype(jnp.float32)
        residual_low = residual.astype(jnp.bfloat16)
        grad_panel = jnp.einsum(
            "ehc,ehr->ecr", residual_low, factor_low, preferred_element_type=jnp.float32
        )
        collected = lax.all_to_all(
            grad_panel.astype(jnp.bfloat16), "expert", split_axis=1, concat_axis=0, tiled=True
        ).astype(grad_panel.dtype)
        grad_rows = factor_gradient(residual_low, panels)
        grad_bases = mix_scale * jnp.einsum(
            "ej,ecr->cjr", mixing_all, collected, precision=lax.Precision.HIGHEST
        )
        partial_mixing = mix_scale * jnp.einsum(
            "cjr,ecr->ej", bases_state, collected, precision=lax.Precision.HIGHEST
        )
        bases_state, bases_one, bases_two = adam_update(
            bases_state, bases_one, bases_two, grad_bases, iteration, EPSILON_BASES
        )
        grad_mixing = lax.psum(partial_mixing, ("expert", "row"))
        mixing_state, mixing_one, mixing_two = adam_update(
            mixing_state, mixing_one, mixing_two, grad_mixing, iteration, EPSILON_MIXING
        )
        factor_state, factor_one, factor_two = adam_update(
            factor_state, factor_one, factor_two, grad_rows, iteration, EPSILON_FACTORS
        )
    mixing_out = lax.dynamic_slice_in_dim(
        mixing_state, lax.axis_index("expert") * local_experts, local_experts, 0
    )
    return (factor_state, bases_state, mixing_out)


def solution(mesh):
    placed = (
        P(("layer", "expert"), None, "row"),
        P(("layer", "expert"), "row", None),
        P(("layer", "expert"), None),
        P(("layer", "row", "expert"), None, None),
    )
    return jax.shard_map(
        body,
        mesh=mesh,
        in_specs=placed,
        out_specs=(
            P(("layer", "expert"), "row", None),
            P(("layer", "row", "expert"), None, None),
            P(("layer", "expert"), None),
        ),
        check_vma=False,
    )
```

profile of v0, /device:TPU:0, one launch (start us, length us, event | category | flops | bytes accessed | tf_op | source)
XLA Modules:
  0.0 272.0 jit_solution(14416674507281021120)
XLA Ops:
  7.2 22.3 %all-gather = f32[8,1,64]{2,1,0:T(1,128)S(1)} all-gather(f32[1,1,64]{2,1,0:T(1,128)} %bitcast.113), channel_id=1, replica_groups=mesh['layer'=2,'expert'=8,'row'=2] {'expert'}, dimensions={0}, use_global_device_ids=true | all-gather | bytes 2304 | tf_op jit(solution)/shard_map/all_gather | solution.py:42
  29.5 0.0 copy-start.2
  29.5 5.8 %fusion.22 = bf16[8,224,128]{2,0,1:T(8,128)(2,1)S(1)} fusion(f32[8,64,1]{1,0,2:T(8,128)S(1)} %bitcast.108, f32[224,64,128]{2,1,0:T(8,128)} %param.7), kind=kOutput, calls=%fused_computation.21 | convolution fusion | flops 176619520 | bytes 7800832 | tf_op jit(solution)/shard_map/ej,cjr->ecr/dot_general | solution.py:56
  35.2 0.8 copy.29
  36.1 3.5 %all-to-all-start = ((bf16[8,224,128]{2,1,0:T(8,128)(2,1)}), bf16[8,224,128]{2,1,0:T(8,128)(2,1)S(1)}, u32[]{:S(2)}, u32[]{:S(2)}) async-start(bf16[8,224,128]{2,1,0:T(8,128)(2,1)} %copy.29), calls=%async_computation | async-start | bytes 917504 | tf_op jit(solution)/shard_map/all_to_all | solution.py:58
  39.6 6.0 %copy.30 = bf16[1,1024,1792]{1,2,0:T(8,128)(2,1)} copy(bf16[1,1024,1792]{2,1,0:T(8,128)(2,1)} %param.4) | data formatting | bytes 7340032 | tf_op args[0]
  45.5 0.0 copy-done.2
  45.5 2.5 all_gather.10
  48.1 1.1 all-to-all-done
  49.1 3.2 %fusion = bf16[1,1024,1792]{1,2,0:T(8,128)(2,1)S(1)} fusion(bf16[1,1024,1792]{1,2,0:T(8,128)(2,1)} %copy.30, bf16[1792,128]{1,0:T(8,128)(2,1)S(1)} %bitcast.100, bf16[1,1024,128]{2,1,0:T(8,128)(2,1)S(1)} %all_gather.10), kind=kOutput, calls=%fused_computation.2 | convolution fusion | flops 475267072 | bytes 8060928 | tf_op jit(solution)/shard_map/ehr,ecr->ehc/dot_general | solution.py:59
  52.3 0.0 copy-start.1
  52.3 1.8 copy-done.1
  54.1 1.1 fusion.19
  55.3 7.1 %copy.55 = bf16[1,1792,128]{2,0,1:T(2,128)(2,1)S(1)} copy(bf16[1,1792,128]{2,1,0:T(8,128)(2,1)S(1)} %fusion.19) | data formatting | bytes 917504 | tf_op jit(solution)/shard_map/convert_element_type | solution.py:67
  62.4 0.5 broadcast.164
  62.9 10.2 %reduce = bf16[1792,128]{1,0:T(8,128)(2,1)S(1)} reduce(bf16[1792,1,128]{2,1,0:T(2,128)(2,1)S(1)} %bitcast.96, bf16[]{:T(256)} %broadcast.164), dimensions={1}, to_apply=%bitcast.91.reduce_sub_computation | reduce | bytes 917506
  73.1 0.9 reshape.68
  73.9 4.9 %all-to-all-start.1 = ((bf16[8,2,14336]{2,1,0:T(2,128)(2,1)}), bf16[8,2,14336]{2,1,0:T(2,128)(2,1)S(1)}, u32[]{:S(2)}, u32[]{:S(2)}) async-start(bf16[8,2,14336]{2,1,0:T(2,128)(2,1)} %reshape.68), calls=%async_computation.2 | async-start | bytes 917504 | tf_op jit(solution)/shard_map/all_to_all | solution.py:66
  78.8 0.2 reduce-scatter.3.cloned.1.call-start
  79.0 3.9 %fusion.33 = bf16[1,1024,128]{2,1,0:T(8,128)(2,1)} fusion(bf16[1792,128]{1,0:T(8,128)(2,1)S(1)} %bitcast.101, bf16[1,1024,1792]{1,2,0:T(8,128)(2,1)} %copy-done.1), kind=kOutput, calls=%fused_computation.26 | convolution fusion | flops 469893120 | bytes 4390912 | tf_op jit(solution)/shard_map/ehc,ecr->ehr/dot_general | solution.py:31
  82.9 0.0 reduce-scatter.3.cloned.1.call-update
  83.0 9.2 %all-to-all-done.1 = bf16[8,2,14336]{2,1,0:T(2,128)(2,1)S(1)} async-done(((bf16[8,2,14336]{2,1,0:T(2,128)(2,1)}), bf16[8,2,14336]{2,1,0:T(2,128)(2,1)S(1)}, u32[]{:S(2)}, u32[]{:S(2)}) %all-to-all-start.1) | async-done | bytes 458784 | tf_op jit(solution)/shard_map/all_to_all | solution.py:66
  92.2 0.5 reshape.69
  92.7 0.0 slice-start
  92.7 0.1 copy.40
  92.7 0.0 slice-start.1
  92.8 12.8 %bitcast_subtract_fusion.1 = (f32[224,64,128]{2,1,0:T(8,128)}, f32[224,128,64]{1,2,0:T(8,128)}) fusion(f32[224,64,128]{2,1,0:T(8,128)} %param.7, f32[8,64,1]{1,0,2:T(8,128)S(1)} %bitcast.109, bf16[8,224,128]{2,1,0:T(8,128)(2,1)S(1)} %bitcast.104), kind=kOutput, calls=%fused_computation.5 | convolution fusion | flops 190840832 | bytes 22480896 | tf_op jit(solution)/shard_map/ej,ecr->cjr/dot_general | solution.py:70
  105.6 0.0 slice-done
  105.6 0.0 slice-done.1
  105.6 3.5 %fusion.37 = f32[8,64]{1,0:T(8,128)S(1)} fusion(f32[224,64,128]{2,1,0:T(8,128)S(1)} %bitcast.93, bf16[8,224,128]{2,1,0:T(8,128)(2,1)S(1)} %bitcast.105), kind=kOutput, calls=%fused_computation.30 | convolution fusion | flops 176161280 | bytes 7800832 | tf_op jit(solution)/shard_map/cjr,ecr->ej/dot_general | solution.py:73
  109.1 31.5 %psum.14 = f32[8,64]{1,0:T(8,128)S(1)} all-reduce(f32[8,64]{1,0:T(8,128)S(1)} %fusion.37), channel_id=1, replica_groups=mesh['layer'=2,'expert'=8,'row'=2] {'expert','row'}, use_global_device_ids=true, to_apply=%region_1.0 | all-reduce | flops 512 | bytes 4096 | tf_op jit(solution)/shard_map/psum | solution.py:79
  140.5 5.7 %fusion.23 = bf16[8,224,128]{2,0,1:T(8,128)(2,1)S(1)} fusion(f32[224,64,128]{2,1,0:T(8,128)} %get-tuple-element.3, f32[8,64]{1,0:T(8,128)S(1)} %bitcast.110, f32[8,64]{1,0:T(8,128)S(1)} %psum.14), kind=kOutput, calls=%fused_computation.22 | convolution fusion | flops 176623104 | bytes 7802880 | tf_op jit(solution)/shard_map/ej,cjr->ecr/dot_general | solution.py:56
  146.3 0.8 copy.34
  147.1 3.5 %all-to-all-start.2 = ((bf16[8,224,128]{2,1,0:T(8,128)(2,1)}), bf16[8,224,128]{2,1,0:T(8,128)(2,1)S(1)}, u32[]{:S(2)}, u32[]{:S(2)}) async-start(bf16[8,224,128]{2,1,0:T(8,128)(2,1)} %copy.34), calls=%async_computation.3 | async-start | bytes 917504 | tf_op jit(solution)/shard_map/all_to_all | solution.py:58
  150.6 0.0 reduce-scatter.3.cloned.1.call-done
  150.6 1.1 fusion.69
  151.7 2.2 all_gather.11
  153.9 8.1 %all-to-all-done.2 = bf16[8,224,128]{2,1,0:T(8,128)(2,1)S(1)} async-done(((bf16[8,224,128]{2,1,0:T(8,128)(2,1)}), bf16[8,224,128]{2,1,0:T(8,128)(2,1)S(1)}, u32[]{:S(2)}, u32[]{:S(2)}) %all-to-all-start.2) | async-done | bytes 458784 | tf_op jit(solution)/shard_map/all_to_all | solution.py:58
  162.0 0.0 copy-start.3
  162.0 3.3 %fusion.1 = bf16[1,1024,1792]{1,2,0:T(8,128)(2,1)S(1)} fusion(bf16[1,1024,1792]{1,2,0:T(8,128)(2,1)} %copy.30, bf16[1792,128]{1,0:T(8,128)(2,1)S(1)} %bitcast.106, bf16[1,1024,128]{2,1,0:T(8,128)(2,1)S(1)} %all_gather.11), kind=kOutput, calls=%fused_computation.3 | convolution fusion | flops 475267072 | bytes 8060928 | tf_op jit(solution)/shard_map/ehr,ecr->ehc/dot_general | solution.py:59
  165.3 0.0 copy-done.3
  165.3 0.0 copy-start
  165.3 1.9 copy-done
  167.2 1.1 fusion.16
  168.3 7.1 %copy.54 = bf16[1,1792,128]{2,0,1:T(2,128)(2,1)S(1)} copy(bf16[1,1792,128]{2,1,0:T(8,128)(2,1)S(1)} %fusion.16) | data formatting | bytes 917504 | tf_op jit(solution)/shard_map/convert_element_type | solution.py:67
  175.5 10.2 %reduce.1 = bf16[1792,128]{1,0:T(8,128)(2,1)S(1)} reduce(bf16[1792,1,128]{2,1,0:T(2,128)(2,1)S(1)} %bitcast.97, bf16[]{:T(256)} %broadcast.164), dimensions={1}, to_apply=%bitcast.90.reduce_sub_computation | reduce | bytes 917506
  185.6 0.9 reshape.70
  186.5 4.1 %all-to-all-start.3 = ((bf16[8,2,14336]{2,1,0:T(2,128)(2,1)}), bf16[8,2,14336]{2,1,0:T(2,128)(2,1)}, u32[]{:S(2)}, u32[]{:S(2)}) async-start(bf16[8,2,14336]{2,1,0:T(2,128)(2,1)} %reshape.70), calls=%async_computation.5 | async-start | bytes 917504 | tf_op jit(solution)/shard_map/all_to_all | solution.py:66
  190.7 0.0 slice-start.2
  190.7 0.3 reduce-scatter.5.cloned.1.call-start
  191.0 4.2 %fusion.30 = bf16[1,1024,128]{2,1,0:T(8,128)(2,1)} fusion(bf16[1792,128]{1,0:T(8,128)(2,1)} %bitcast.107, bf16[1,1024,1792]{1,2,0:T(8,128)(2,1)} %copy-done), kind=kOutput, calls=%fused_computation.25 | convolution fusion | flops 469893120 | bytes 4390912 | tf_op jit(solution)/shard_map/ehc,ecr->ehr/dot_general | solution.py:31
  195.1 0.0 reduce-scatter.5.cloned.1.call-update
  195.2 9.1 %reduce-scatter.5.cloned.1.call-done = bf16[1,512,128]{2,1,0:T(8,128)(2,1)} async-done(((bf16[1,1024,128]{2,1,0:T(8,128)(2,1)}), bf16[1,512,128]{2,1,0:T(8,128)(2,1)}) %reduce-scatter.5.cloned.1.call-update) | async-done | bytes 131088 | tf_op jit(solution)/shard_map/reduce_scatter | solution.py:34
  204.3 0.0 copy-done.4
  204.3 1.9 fusion.54
  206.2 0.0 all-to-all-done.3
  206.2 3.4 %reshape.71 = bf16[1792,1,128]{2,1,0:T(2,128)(2,1)} reshape(bf16[8,2,14336]{2,1,0:T(2,128)(2,1)} %all-to-all-done.3) | data formatting | bytes 917504
  209.6 1.4 copy.41
  211.0 6.8 %fusion.36 = f32[8,64]{1,0:T(8,128)S(1)} fusion(f32[224,64,128]{2,1,0:T(8,128)} %get-tuple-element.3, bf16[8,224,128]{2,1,0:T(8,128)(2,1)S(1)} %bitcast.102), kind=kOutput, calls=%fused_computation.28 | convolution fusion | flops 176161280 | bytes 7800832 | tf_op jit(solution)/shard_map/cjr,ecr->ej/dot_general | solution.py:73
  217.8 0.0 slice-done.2
  217.8 0.0 slice-done.3
  217.8 12.7 %bitcast_subtract_fusion = f32[224,64,128]{2,1,0:T(8,128)} fusion(f32[224,64,128]{2,1,0:T(8,128)S(1)} %bitcast.95, f32[224,128,64]{1,2,0:T(8,128)} %get-tuple-element.4, bf16[8,224,128]{2,1,0:T(8,128)(2,1)S(1)} %bitcast.103, f32[8,64]{1,0:T(8,128)S(1)} %bitcast.111, f32[8,64]{1,0:T(8,128)S(1)} %psum.14), kind=kOutput, calls=%fused_computation.4 | convolution fusion | flops 205524480 | bytes 22482944 | tf_op jit(solution)/shard_map/ej,ecr->cjr/dot_general | solution.py:70
  230.5 33.8 %psum.15 = f32[8,64]{1,0:T(8,128)S(1)} all-reduce(f32[8,64]{1,0:T(8,128)S(1)} %fusion.36), channel_id=1, replica_groups=mesh['layer'=2,'expert'=8,'row'=2] {'expert','row'}, use_global_device_ids=true, to_apply=%region_3.0 | all-reduce | flops 512 | bytes 4096 | tf_op jit(solution)/shard_map/psum | solution.py:79
  264.4 0.5 constant_dynamic-slice_fusion
  (6 shorter events, 0.0 us)
Async XLA Ops:
  29.5 16.1 %copy-start.2 = (f32[1,512,128]{2,1,0:T(8,128)S(1)}, f32[1,512,128]{2,1,0:T(8,128)}, u32[]{:S(2)}) copy-start(f32[1,512,128]{2,1,0:T(8,128)} %param.5) | copy-start | bytes 786436
  36.1 13.1 %all-to-all-start = ((bf16[8,224,128]{2,1,0:T(8,128)(2,1)}), bf16[8,224,128]{2,1,0:T(8,128)(2,1)S(1)}, u32[]{:S(2)}, u32[]{:S(2)}) async-start(bf16[8,224,128]{2,1,0:T(8,128)(2,1)} %copy.29), calls=%async_computation | async-start | bytes 917504 | tf_op jit(solution)/shard_map/all_to_all | solution.py:58
  52.3 1.8 copy-start.1
  73.9 18.2 %all-to-all-start.1 = ((bf16[8,2,14336]{2,1,0:T(2,128)(2,1)}), bf16[8,2,14336]{2,1,0:T(2,128)(2,1)S(1)}, u32[]{:S(2)}, u32[]{:S(2)}) async-start(bf16[8,2,14336]{2,1,0:T(2,128)(2,1)} %reshape.68), calls=%async_computation.2 | async-start | bytes 917504 | tf_op jit(solution)/shard_map/all_to_all | solution.py:66
  78.8 71.8 %reduce-scatter.3.cloned.1.call-start = ((), (), s32[]{:S(2)}) async-start(), calls=%async_computation.6 | async-start | bytes 393216 | tf_op jit(solution)/shard_map/reduce_scatter | solution.py:34
  92.7 12.9 %slice-start = ((s8[7340032]{0:T(1024)(128)(4,1)}), s8[4194304]{0:T(1024)(128)(4,1)S(1)}, s32[]{:S(2)}) async-start(s8[7340032]{0:T(1024)(128)(4,1)} %bitcast.92), calls=%async_computation.8 | async-start | bytes 8388608
  92.7 12.8 %slice-start.1 = ((s8[7340032]{0:T(1024)(128)(4,1)}), s8[3145728]{0:T(1024)(128)(4,1)S(1)}, s32[]{:S(2)}) async-start(s8[7340032]{0:T(1024)(128)(4,1)} %bitcast.92), calls=%async_computation.9 | async-start | bytes 6291456
  147.1 14.9 %all-to-all-start.2 = ((bf16[8,224,128]{2,1,0:T(8,128)(2,1)}), bf16[8,224,128]{2,1,0:T(8,128)(2,1)S(1)}, u32[]{:S(2)}, u32[]{:S(2)}) async-start(bf16[8,224,128]{2,1,0:T(8,128)(2,1)} %copy.34), calls=%async_computation.3 | async-start | bytes 917504 | tf_op jit(solution)/shard_map/all_to_all | solution.py:58
  162.0 3.3 %copy-start.3 = (bf16[8,224,128]{2,1,0:T(8,128)(2,1)}, bf16[8,224,128]{2,1,0:T(8,128)(2,1)S(1)}, u32[]{:S(2)}) copy-start(bf16[8,224,128]{2,1,0:T(8,128)(2,1)S(1)} %all-to-all-done.2) | copy-start | bytes 1376260
  165.3 1.9 copy-start
  167.2 37.1 %copy-start.4 = (bf16[1,512,128]{2,1,0:T(8,128)(2,1)S(1)}, bf16[1,512,128]{2,1,0:T(8,128)(2,1)}, u32[]{:S(2)}) copy-start(bf16[1,512,128]{2,1,0:T(8,128)(2,1)} %reduce-scatter.3.cloned.1.call-done) | copy-start | bytes 393220
  186.5 19.7 %all-to-all-start.3 = ((bf16[8,2,14336]{2,1,0:T(2,128)(2,1)}), bf16[8,2,14336]{2,1,0:T(2,128)(2,1)}, u32[]{:S(2)}, u32[]{:S(2)}) async-start(bf16[8,2,14336]{2,1,0:T(2,128)(2,1)} %reshape.70), calls=%async_computation.5 | async-start | bytes 917504 | tf_op jit(solution)/shard_map/all_to_all | solution.py:66
  190.7 27.1 %slice-start.2 = ((s8[7340032]{0:T(1024)(128)(4,1)}), s8[3145728]{0:T(1024)(128)(4,1)S(1)}, s32[]{:S(2)}) async-start(s8[7340032]{0:T(1024)(128)(4,1)} %bitcast.94), calls=%async_computation.10 | async-start | bytes 6291456
  190.7 13.6 %reduce-scatter.5.cloned.1.call-start = ((), (), s32[]{:S(2)}) async-start(), calls=%async_computation.7 | async-start | bytes 393216 | tf_op jit(solution)/shard_map/reduce_scatter | solution.py:34
  209.6 8.2 %slice-start.3 = ((s8[7340032]{0:T(1024)(128)(4,1)}), s8[4194304]{0:T(1024)(128)(4,1)S(1)}, s32[]{:S(2)}) async-start(s8[7340032]{0:T(1024)(128)(4,1)} %bitcast.94), calls=%async_computation.11 | async-start | bytes 8388608
Sparse Core Ops, SparseCore 0:
  83.1 9.0 reduce-scatter.2
  195.3 8.9 reduce-scatter.4
where the time goes:
time: 275 us; the launch traced here: 272 us
  blocking collectives  92.3 us (34%)
  matrix products  64 us (23%)
  local copies, waits for them, and re-layouts  33.8 us (12%)
  waiting for transfers between devices  27.6 us (10%)
  other arithmetic  23.4 us (9%)
  starting transfers between devices  16.4 us (6%)
  between operations  14.5 us (5%)
    psum x2, blocking collectives, body(): grad_mixing = lax.psum(partial_mixing, ('expert', 'row'))  65.3 us
    dot_general x2, matrix products, body(): jnp.einsum('ej,ecr->cjr', mixing_all, collected, precision=lax.Precision....  25.5 us
    all_gather x1, blocking collectives, body(): mixing_state = lax.all_gather(mixing, 'expert', axis=0, tiled=True)  22.3 us
    unnamed x4, other arithmetic  20.3 us
    unnamed x26, local copies, waits for them, and re-layouts  17.4 us
    convert_element_type x2, local copies, waits for them, and re-layouts, body(): grad_panel.astype(jnp.bfloat16)  14.3 us
    dot_general x2, matrix products, body(): jnp.einsum('ej,cjr->ecr', mixing_all, bases_state, precision=lax.Precisio...  11.5 us
    dot_general x2, matrix products, body(): jnp.einsum('cjr,ecr->ej', bases_state, collected, precision=lax.Precision...  10.3 us
  transfers between devices with their start and end apart: 6, of which 4 were waited for; matrix products, arithmetic and copies ran while one was open for 15% of the time, Pallas kernels for 0%

commit v1 on v0

--- a/solution.py
+++ b/solution.py
@@ -1,8 +1,11 @@
+import functools
 import math
 
 import jax
 import jax.numpy as jnp
 from jax import lax
+from jax.experimental import pallas as pl
+from jax.experimental.pallas import tpu as pltpu
 from jax.sharding import PartitionSpec as P
 
 ITERS = 2
@@ -14,6 +17,15 @@
 EPSILON_FACTORS = 8.0
 EPSILON_BASES = 6.0
 EPSILON_MIXING = 300.0
+
+FIRST_OLD = BETA_ONE * (1.0 - BETA_ONE) / (1.0 - BETA_ONE**2)
+FIRST_NEW = (1.0 - BETA_ONE) / (1.0 - BETA_ONE**2)
+SECOND_OLD = BETA_TWO * (1.0 - BETA_TWO) / (1.0 - BETA_TWO**2)
+SECOND_NEW = (1.0 - BETA_TWO) / (1.0 - BETA_TWO**2)
+
+GROUP = 16
+CHUNK = 32
+MEGABYTE = 1 << 20
 
 
 def adam_update(values, moment_one, moment_two, gradient, iteration, epsilon):
@@ -27,6 +39,366 @@
     return (values, moment_one, moment_two)
 
 
+def first_step(values, gradient, epsilon):
+    return values - RATE * gradient / (jnp.abs(gradient) + epsilon)
+
+
+def second_step(values, old, new, epsilon):
+    values = first_step(values, old, epsilon)
+    top = FIRST_OLD * old + FIRST_NEW * new
+    root = jnp.sqrt(SECOND_OLD * (old * old) + SECOND_NEW * (new * new))
+    return values - RATE * top / (root + epsilon)
+
+
+def halves(array):
+    high = array.astype(jnp.bfloat16)
+    low = (array - high.astype(jnp.float32)).astype(jnp.bfloat16)
+    return (high, low)
+
+
+def dot(left, right, contract=((1,), (0,))):
+    return lax.dot_general(left, right, (contract, ((), ())), preferred_element_type=jnp.float32)
+
+
+def spread_rows(mixing, scale):
+    experts, bases = mixing.shape
+    rows, columns = experts * GROUP, GROUP * bases
+    pick = (
+        lax.broadcasted_iota(jnp.int32, (rows, experts), 0) // GROUP
+        == lax.broadcasted_iota(jnp.int32, (rows, experts), 1)
+    ).astype(jnp.bfloat16)
+    tile = (
+        lax.broadcasted_iota(jnp.int32, (bases, columns), 0)
+        == lax.broadcasted_iota(jnp.int32, (bases, columns), 1) % bases
+    ).astype(jnp.bfloat16)
+    keep = (
+        lax.broadcasted_iota(jnp.int32, (rows, columns), 0) % GROUP
+        == lax.broadcasted_iota(jnp.int32, (rows, columns), 1) // bases
+    )
+    parts = []
+    for half in halves(scale * mixing):
+        wide = dot(half, tile).astype(jnp.bfloat16)
+        parts.append(jnp.where(keep, dot(pick, wide), 0.0).astype(jnp.bfloat16))
+    return jnp.concatenate(parts, axis=0)
+
+
+def spread_columns(mixing, scale):
+    experts, bases = mixing.shape
+    rows, columns = GROUP * bases, experts * GROUP
+    pick = (
+        lax.broadcasted_iota(jnp.int32, (experts, columns), 0)
+        == lax.broadcasted_iota(jnp.int32, (experts, columns), 1) // GROUP
+    ).astype(jnp.bfloat16)
+    tile = (
+        lax.broadcasted_iota(jnp.int32, (rows, bases), 0) % bases
+        == lax.broadcasted_iota(jnp.int32, (rows, bases), 1)
+    ).astype(jnp.bfloat16)
+    keep = (
+        lax.broadcasted_iota(jnp.int32, (rows, columns), 0) // bases
+        == lax.broadcasted_iota(jnp.int32, (rows, columns), 1) % GROUP
+    )
+    parts = []
+    for half in halves(scale * mixing):
+        wide = dot(half, pick, ((0,), (0,))).astype(jnp.bfloat16)
+        parts.append(jnp.where(keep, dot(tile, wide), 0.0).astype(jnp.bfloat16))
+    return jnp.concatenate(parts, axis=1)
+
+
+def call(kernel, out_shape, *args, grid=(), in_specs=None, out_specs=None, scratch=(), flops=0, traffic=0, limit=40):
+    whole = pl.BlockSpec(memory_space=pltpu.VMEM)
+    single = isinstance(out_shape, jax.ShapeDtypeStruct)
+    return pl.pallas_call(
+        kernel,
+        out_shape=out_shape,
+        grid=grid,
+        in_specs=[whole] * len(args) if in_specs is None else in_specs,
+        out_specs=(whole if single else [whole] * len(out_shape)) if out_specs is None else out_specs,
+        scratch_shapes=list(scratch),
+        compiler_params=pltpu.CompilerParams(vmem_limit_bytes=limit * MEGABYTE),
+        cost_estimate=pl.CostEstimate(flops=flops, bytes_accessed=traffic, transcendentals=0),
+    )(*args)
+
+
+def shape_of(shape, dtype):
+    return jax.ShapeDtypeStruct(tuple(shape), dtype)
+
+
+def store_products(weights_ref, low, product_ref, gram_ref):
+    product_ref[...] = dot(low, weights_ref[...], ((0,), (0,))).T
+    gram_ref[...] = dot(low, low, ((0,), (0,)))
+
+
+def start_kernel(row_ref, weights_ref, own_ref, other_ref, full_ref, low_ref, product_ref, gram_ref):
+    rows = own_ref.shape[0]
+    row = row_ref[0]
+    full_ref[pl.ds(pl.multiple_of(row * rows, rows), rows), :] = own_ref[...]
+    full_ref[pl.ds(pl.multiple_of((1 - row) * rows, rows), rows), :] = other_ref[...]
+    low = full_ref[...].astype(jnp.bfloat16)
+    low_ref[...] = low
+    store_products(weights_ref, low, product_ref, gram_ref)
+
+
+def step_kernel(weights_ref, full_ref, mine_ref, other_ref, low_ref, product_ref, gram_ref):
+    gradient = mine_ref[...].astype(jnp.float32) + other_ref[...].astype(jnp.float32)
+    low = first_step(full_ref[...], gradient, EPSILON_FACTORS).astype(jnp.bfloat16)
+    low_ref[...] = low
+    store_products(weights_ref, low, product_ref, gram_ref)
+
+
+def panel_kernel(panels_ref, product_ref, gram_ref, out_ref):
+    high, low = halves(gram_ref[...])
+    panels = panels_ref[...]
+    out_ref[...] = (dot(panels, high) + dot(panels, low) - product_ref[...]).astype(jnp.bfloat16)
+
+
+def factor_kernel(weights_ref, low_ref, panels_ref, out_ref):
+    panels = panels_ref[...]
+    high, low = halves(dot(panels, panels, ((0,), (0,))))
+    factors = low_ref[...]
+    out_ref[...] = (
+        dot(factors, high) + dot(factors, low) - dot(weights_ref[...], panels)
+    ).astype(jnp.bfloat16)
+
+
+def last_factor_kernel(row_ref, own_ref, mine_old_ref, other_old_ref, mine_ref, other_ref, out_ref):
+    rows = own_ref.shape[0]
+    here = pl.ds(pl.multiple_of(row_ref[0] * rows, rows), rows)
+    old = mine_old_ref[here, :].astype(jnp.float32) + other_old_ref[here, :].astype(jnp.float32)
+    new = mine_ref[here, :].astype(jnp.float32) + other_ref[here, :].astype(jnp.float32)
+    out_ref[...] = second_step(own_ref[...], old, new, EPSILON_FACTORS)
+
+
+def group_of(ref, position):
+    block = ref[position * GROUP : (position + 1) * GROUP]
+    return block.reshape(-1, block.shape[-1])
+
+
+def blocks_of(ref, position):
+    block = ref[:, position * GROUP : (position + 1) * GROUP, :]
+    return block.reshape(-1, block.shape[-1])
+
+
+def mix_groups(spread, bases_ref, out_ref):
+    half = spread.shape[0] // 2
+    for position in range(bases_ref.shape[0] // GROUP):
+        both = dot(spread, group_of(bases_ref, position).astype(jnp.bfloat16))
+        mixed = (both[:half] + both[half:]).astype(jnp.bfloat16)
+        out_ref[:, position * GROUP : (position + 1) * GROUP, :] = mixed.reshape(-1, GROUP, mixed.shape[-1])
+
+
+def mix_kernel(scale, mixing_ref, bases_ref, out_ref, spread):
+    @pl.when(pl.program_id(0) == 0)
+    def _():
+        spread[...] = spread_rows(mixing_ref[...], scale)
+
+    mix_groups(spread[...], bases_ref, out_ref)
+
+
+def next_mix_kernel(scale, sums_ref, mixing_ref, bases_ref, out_ref, next_ref, grad_ref, spread):
+    @pl.when(pl.program_id(0) == 0)
+    def _():
+        gradient = jnp.sum(sums_ref[...], axis=0)
+        following = first_step(mixing_ref[...], gradient, EPSILON_MIXING)
+        next_ref[...] = following
+        grad_ref[...] = gradient
+        spread[...] = spread_rows(following, scale)
+
+    mix_groups(spread[...], bases_ref, out_ref)
+
+
+def mixing_kernel(scale, bases_ref, blocks_ref, out_ref, total):
+    step = pl.program_id(0)
+
+    @pl.when(step == 0)
+    def _():
+        total[...] = jnp.zeros_like(total)
+
+    count = bases_ref.shape[0] // GROUP
+    left = jnp.concatenate([blocks_of(blocks_ref, position) for position in range(count)], axis=1)
+    right = jnp.concatenate(
+        [group_of(bases_ref, position).astype(jnp.bfloat16) for position in range(count)], axis=1
+    )
+    total[...] += dot(left, right, ((1,), (1,)))
+
+    @pl.when(step == pl.num_programs(0) - 1)
+    def _():
+        rows, columns = total.shape
+        experts, bases = rows // GROUP, columns // GROUP
+        keep = (
+            lax.broadcasted_iota(jnp.int32, (rows, columns), 0) % GROUP
+            == lax.broadcasted_iota(jnp.int32, (rows, columns), 1) // bases
+        )
+        wide = jnp.where(keep, total[...], 0.0).reshape(experts, GROUP, columns).sum(axis=1)
+        fold = (
+            lax.broadcasted_iota(jnp.int32, (columns, bases), 0) % bases
+            == lax.broadcasted_iota(jnp.int32, (columns, bases), 1)
+        ).astype(jnp.float32)
+        gradient = scale * lax.dot_general(
+            wide, fold, (((1,), (0,)), ((), ())),
+            precision=lax.Precision.HIGHEST, preferred_element_type=jnp.float32,
+        )
+        out_ref[...] = jnp.broadcast_to(gradient[None], out_ref.shape)
+
+
+def gradient_group(spread, blocks_ref, position):
+    blocks = blocks_of(blocks_ref, position)
+    return dot(spread, jnp.concatenate([blocks, blocks], axis=0))
+
+
+def base_kernel(scale, mixing_ref, bases_ref, blocks_ref, out_ref, spread):
+    @pl.when(pl.program_id(0) == 0)
+    def _():
+        spread[...] = spread_columns(mixing_ref[...], scale)
+
+    for position in range(bases_ref.shape[0] // GROUP):
+        gradient = gradient_group(spread[...], blocks_ref, position)
+        values = first_step(group_of(bases_ref, position), gradient, EPSILON_BASES)
+        out_ref[position * GROUP : (position + 1) * GROUP] = values.astype(out_ref.dtype).reshape(
+            GROUP, -1, values.shape[-1]
+        )
+
+
+def last_base_kernel(
+    scale, old_ref, new_ref, bases_ref, old_blocks_ref, blocks_ref, out_ref, old_spread, spread
+):
+    @pl.when(pl.program_id(0) == 0)
+    def _():
+        old_spread[...] = spread_columns(old_ref[...], scale)
+        spread[...] = spread_columns(new_ref[...], scale)
+
+    for position in range(bases_ref.shape[0] // GROUP):
+        old = gradient_group(old_spread[...], old_blocks_ref, position)
+        new = gradient_group(spread[...], blocks_ref, position)
+        values = second_step(group_of(bases_ref, position), old, new, EPSILON_BASES)
+        out_ref[position * GROUP : (position + 1) * GROUP] = values.reshape(GROUP, -1, values.shape[-1])
+
+
+def swap_rows(array):
+    return lax.ppermute(array, "row", [(0, 1), (1, 0)])
+
+
+def exchange(array):
+    return lax.all_to_all(array, "expert", split_axis=0, concat_axis=0, tiled=True)
+
+
+def kernel_body(weights, factors, mixing, shared_bases):
+    bf16, f32 = jnp.bfloat16, jnp.float32
+    weights = weights[0]
+    factors = factors[0]
+    height, width = weights.shape
+    own_rows, rank = factors.shape
+    columns, bases, _ = shared_bases.shape
+    experts = width // columns
+    devices = experts * (height // own_rows)
+    scale = 1.0 / math.sqrt(bases * rank)
+    row = lax.axis_index("row").reshape(1)
+    expert = lax.axis_index("expert")
+    scalar = pl.BlockSpec(memory_space=pltpu.SMEM)
+    whole = pl.BlockSpec(memory_space=pltpu.VMEM)
+
+    wide_flops = 2 * height * width * rank
+    mix_flops = 2 * columns * GROUP * experts * bases * rank
+    block_bytes = 2 * width * rank
+    base_bytes = 4 * shared_bases.size
+
+    steps = columns // CHUNK
+    bases_spec = pl.BlockSpec((CHUNK, bases, rank), lambda s: (s, 0, 0))
+    blocks_spec = pl.BlockSpec((experts, CHUNK, rank), lambda s: (0, s, 0))
+
+    def fixed(*shape):
+        return pl.BlockSpec(shape, lambda s: (0,) * len(shape))
+
+    blocks = shape_of((experts, columns, rank), bf16)
+    panels_shape = shape_of((width, rank), bf16)
+    small = shape_of((experts, bases), f32)
+    rows_spread = pltpu.VMEM((2 * experts * GROUP, GROUP * bases), bf16)
+    columns_spread = pltpu.VMEM((GROUP * bases, 2 * experts * GROUP), bf16)
+    products = [shape_of((height, rank), bf16), shape_of((width, rank), f32), shape_of((rank, rank), f32)]
+
+    def factor_part(low, panels):
+        return call(
+            factor_kernel, shape_of((height, rank), bf16), weights, low, panels,
+            flops=wide_flops, traffic=weights.size * 2 + block_bytes,
+        )
+
+    def panel_part(panels, product, gram):
+        return call(
+            panel_kernel, panels_shape, panels, product, gram, flops=wide_flops // 8, traffic=4 * block_bytes
+        ).reshape(blocks.shape)
+
+    def mixing_part(values, collected):
+        return call(
+            functools.partial(mixing_kernel, scale),
+            shape_of((devices, experts, bases), f32), values, collected,
+            grid=(steps,), in_specs=[bases_spec, blocks_spec],
+            out_specs=fixed(devices, experts, bases),
+            scratch=[pltpu.VMEM((experts * GROUP, GROUP * bases), f32)],
+            flops=mix_flops, traffic=values.size * values.dtype.itemsize,
+        )
+
+    other = swap_rows(factors)
+    mixing_all = exchange(jnp.broadcast_to(mixing, (experts, bases)))
+    full, low_one, product_one, gram_one = call(
+        start_kernel, [shape_of((height, rank), f32)] + products, row, weights, factors, other,
+        in_specs=[scalar, whole, whole, whole],
+        flops=wide_flops, traffic=weights.size * 2 + 4 * block_bytes,
+    )
+
+    mixed_one = call(
+        functools.partial(mix_kernel, scale), blocks, mixing_all, shared_bases,
+        grid=(steps,), in_specs=[fixed(experts, bases), bases_spec], out_specs=blocks_spec,
+        scratch=[rows_spread], flops=2 * mix_flops, traffic=base_bytes,
+    )
+    panels_one = exchange(mixed_one).reshape(width, rank)
+    collected_one = exchange(panel_part(panels_one, product_one, gram_one))
+    mine_one = factor_part(low_one, panels_one)
+    other_one = swap_rows(mine_one)
+    low_two, product_two, gram_two = call(
+        step_kernel, products, weights, full, mine_one, other_one,
+        flops=wide_flops, traffic=weights.size * 2 + 4 * block_bytes,
+    )
+    partial_one = mixing_part(shared_bases, collected_one)
+    sums_one = lax.all_to_all(partial_one, ("expert", "row"), split_axis=0, concat_axis=0, tiled=True)
+    bases_one = call(
+        functools.partial(base_kernel, scale), shape_of(shared_bases.shape, bf16),
+        mixing_all, shared_bases, collected_one,
+        grid=(steps,), in_specs=[fixed(experts, bases), bases_spec, blocks_spec], out_specs=bases_spec,
+        scratch=[columns_spread], flops=2 * mix_flops, traffic=2 * base_bytes,
+    )
+
+    mixed_two, mixing_one, grad_one = call(
+        functools.partial(next_mix_kernel, scale), [blocks, small, small], sums_one, mixing_all, bases_one,
+        grid=(steps,),
+        in_specs=[fixed(devices, experts, bases), fixed(experts, bases), bases_spec],
+        out_specs=[blocks_spec, fixed(experts, bases), fixed(experts, bases)],
+        scratch=[rows_spread], flops=2 * mix_flops, traffic=base_bytes // 2,
+    )
+    panels_two = exchange(mixed_two).reshape(width, rank)
+    collected_two = exchange(panel_part(panels_two, product_two, gram_two))
+    mine_two = factor_part(low_two, panels_two)
+    other_two = swap_rows(mine_two)
+    factors_new = call(
+        last_factor_kernel, shape_of((own_rows, rank), f32),
+        row, factors, mine_one, other_one, mine_two, other_two,
+        in_specs=[scalar] + [whole] * 5, traffic=12 * own_rows * rank,
+    )
+    partial_two = mixing_part(bases_one, collected_two)
+    sums_two = lax.all_to_all(partial_two, ("expert", "row"), split_axis=0, concat_axis=0, tiled=True)
+    bases_new = call(
+        functools.partial(last_base_kernel, scale), shape_of(shared_bases.shape, f32),
+        mixing_all, mixing_one, shared_bases, collected_one, collected_two,
+        grid=(steps,),
+        in_specs=[fixed(experts, bases)] * 2 + [bases_spec, blocks_spec, blocks_spec],
+        out_specs=bases_spec,
+        scratch=[columns_spread, columns_spread], flops=4 * mix_flops, traffic=2 * base_bytes,
+    )
+    grad_two = lax.dynamic_slice_in_dim(jnp.sum(sums_two, axis=0), expert, 1, 0)
+    mixing_new = second_step(
+        mixing, lax.dynamic_slice_in_dim(grad_one, expert, 1, 0), grad_two, EPSILON_MIXING
+    )
+    return (factors_new[None], bases_new, mixing_new)
+
+
 def factor_gradient(residual_low, panels):
     grad_factor = jnp.einsum(
         "ehc,ecr->ehr", residual_low, panels, preferred_element_type=jnp.float32
@@ -36,7 +408,7 @@
     ).astype(jnp.float32)
 
 
-def body(weights, factors, mixing, shared_bases):
+def plain_body(weights, factors, mixing, shared_bases):
     mix_scale = 1.0 / math.sqrt(shared_bases.shape[1] * shared_bases.shape[2])
     local_experts = mixing.shape[0]
     mixing_state = lax.all_gather(mixing, "expert", axis=0, tiled=True)
@@ -89,6 +461,21 @@
     return (factor_state, bases_state, mixing_out)
 
 
+def body(weights, factors, mixing, shared_bases):
+    columns, bases, rank = shared_bases.shape
+    experts = weights.shape[2] // columns
+    fits = (
+        weights.shape[0] == 1
+        and weights.shape[1] == 2 * factors.shape[1]
+        and columns % CHUNK == 0
+        and experts == 8
+        and bases == 64
+        and rank == 128
+    )
+    run = kernel_body if fits else plain_body
+    return run(weights, factors, mixing, shared_bases)
+
+
 def solution(mesh):
     placed = (
         P(("layer", "expert"), None, "row"),

time: 275 us -> 143 us (0.52)
  matrix products: 64 us -> 0 us
  blocking collectives: 92.3 us -> 29.6 us
  Pallas kernels: 0 us -> 35.7 us
  other arithmetic: 23.4 us -> 2.06 us
  between operations: 14.5 us -> 0.82 us
  local copies, waits for them, and re-layouts: 33.8 us -> 29 us
  starting transfers between devices: 16.4 us -> 20.6 us
  waiting for transfers between devices: 27.6 us -> 24.5 us
    psum x2 -> x0, blocking collectives: 65.3 us -> none  [body(): grad_mixing = lax.psum(partial_mixing, ('expert', 'row'))]
    dot_general x12 -> x0, matrix products: 64 us -> none  [the longest x2 25.5 us: body(): jnp.einsum('ej,ecr->cjr', mixing_all, collected, precision=lax.Precision....]
    pallas_call x0 -> x13, Pallas kernels: none -> 35.7 us  [call(): pl.pallas_call(kernel, out_shape=out_shape, grid=grid, in_specs=[whole] *...]
    all_to_all x0 -> x2, blocking collectives: none -> 29.6 us  [exchange(): lax.all_to_all(array, 'expert', split_axis=0, concat_axis=0, tiled=True)]
    all_gather x3 -> x0, blocking collectives: 27 us -> none  [the longest x1 22.3 us: body(): mixing_state = lax.all_gather(mixing, 'expert', axis=0, tiled=True)]
    unnamed x4 -> x0, other arithmetic: 20.3 us -> none
    convert_element_type x4 -> x0, local copies, waits for them, and re-layouts: 15.9 us -> none  [the longest x2 14.3 us: body(): grad_panel.astype(jnp.bfloat16)]
    unnamed x26 -> x32, local copies, waits for them, and re-layouts: 17.4 us -> 27.8 us
  transfers between devices with their start and end apart: 6 -> 8, of which waited for: 4 -> 6; matrix products, arithmetic and copies ran while one was open for 15% -> 0% of each run, Pallas kernels for 0% -> 13%
where the time goes in v1:
time: 143 us; the launch traced here: 142 us
  Pallas kernels  35.7 us (25%)
  blocking collectives  29.6 us (21%)
  local copies, waits for them, and re-layouts  29 us (20%)
  waiting for transfers between devices  24.5 us (17%)
  starting transfers between devices  20.6 us (14%)
  other arithmetic  2.06 us (1%)
    pallas_call x13, Pallas kernels, call(): pl.pallas_call(kernel, out_shape=out_shape, grid=grid, in_specs=[whole] *...  35.7 us
    all_to_all x2, blocking collectives, exchange(): lax.all_to_all(array, 'expert', split_axis=0, concat_axis=0, tiled=True)  29.6 us
    unnamed x32, local copies, waits for them, and re-layouts  27.8 us
    all_to_all x3, waiting for transfers between devices, exchange(): lax.all_to_all(array, 'expert', split_axis=0, concat_axis=0, tiled=True)  19.9 us
    all_to_all x3, starting transfers between devices, exchange(): lax.all_to_all(array, 'expert', split_axis=0, concat_axis=0, tiled=True)  13 us
    ppermute x3, waiting for transfers between devices, swap_rows(): return lax.ppermute(array, 'row', [(0, 1), (1, 0)])  4.56 us
    all_to_all x1, starting transfers between devices, kernel_body(): lax.all_to_all(partial_two, ('expert', 'row'), split_axis=0, concat_axis=...  3.74 us
    all_to_all x1, starting transfers between devices, kernel_body(): lax.all_to_all(partial_one, ('expert', 'row'), split_axis=0, concat_axis=...  3.6 us
  transfers between devices with their start and end apart: 8, of which 6 were waited for; matrix products, arithmetic and copies ran while one was open for 0% of the time, Pallas kernels for 13%

profile of v1, /device:TPU:0, one launch (start us, length us, event | category | flops | bytes accessed | tf_op | source)
XLA Modules:
  0.0 142.2 jit_solution(10479635883761272143)
XLA Ops:
  0.6 0.7 broadcast_in_dim.8
  1.3 13.5 %all_to_all.38 = f32[8,1,64]{2,1,0:T(1,128)S(1)} all-to-all(f32[8,1,64]{2,1,0:T(1,128)S(1)} %broadcast_in_dim.8), channel_id=1, replica_groups=mesh['layer'=2,'expert'=8,'row'=2] {'expert'}, dimensions={0} | all-to-all | bytes 4096 | tf_op jit(solution)/shard_map/all_to_all | solution.py:281
  14.8 0.0 copy-start
  14.8 3.1 %copy-done = f32[224,64,128]{2,1,0:T(8,128)S(1)} copy-done((f32[224,64,128]{2,1,0:T(8,128)S(1)}, f32[224,64,128]{2,1,0:T(8,128)}, u32[]{:S(2)}) %copy-start) | copy-done | bytes 7340056
  17.9 0.0 copy-start.10
  17.9 4.8 %shard_map.71 = bf16[8,224,128]{2,1,0:T(8,128)(2,1)} custom-call(f32[8,64]{1,0:T(8,128)S(1)} %bitcast.22, f32[224,64,128]{2,1,0:T(8,128)S(1)} %copy-done), custom_call_target="tpu_custom_call" | custom-call | flops 939524096 | bytes 7340032 | tf_op jit(solution)/shard_map/pallas_call | solution.py:110
  22.7 3.5 %all-to-all-start.1 = ((bf16[8,224,128]{2,1,0:T(8,128)(2,1)}), bf16[8,224,128]{2,1,0:T(8,128)(2,1)S(1)}, u32[]{:S(2)}, u32[]{:S(2)}) async-start(bf16[8,224,128]{2,1,0:T(8,128)(2,1)} %shard_map.71), calls=%async_computation.1 | async-start | bytes 917504 | tf_op jit(solution)/shard_map/all_to_all | solution.py:281
  26.1 0.0 copy-done.10
  26.1 0.1 collective-permute-start
  26.2 1.5 %collective-permute-done.other_ref = f32[512,128]{1,0:T(8,128)S(1)} collective-permute-done((f32[512,128]{1,0:T(8,128)S(1)}, f32[512,128]{1,0:T(8,128)S(1)}, u32[]{:S(2)}, u32[]{:S(2)}) %collective-permute-start) | collective-permute-done | bytes 262176 | tf_op jit(solution)/shard_map/ppermute | solution.py:277
  27.8 0.0 copy-start.4
  27.8 2.0 %copy-done.4 = bf16[1,1024,1792]{2,1,0:T(8,128)(2,1)S(1)} copy-done((bf16[1,1024,1792]{2,1,0:T(8,128)(2,1)S(1)}, bf16[1,1024,1792]{2,1,0:T(8,128)(2,1)}, u32[]{:S(2)}) %copy-start.4) | copy-done | bytes 3670040
  29.8 0.9 shard_map.70
  30.7 0.0 copy-start.11
  30.7 0.8 copy-done.11
  31.5 6.5 %all-to-all-done.1 = bf16[8,224,128]{2,1,0:T(8,128)(2,1)S(1)} async-done(((bf16[8,224,128]{2,1,0:T(8,128)(2,1)}), bf16[8,224,128]{2,1,0:T(8,128)(2,1)S(1)}, u32[]{:S(2)}, u32[]{:S(2)}) %all-to-all-start.1) | async-done | bytes 458784 | tf_op jit(solution)/shard_map/all_to_all | solution.py:281
  38.0 0.4 shard_map.74
  38.4 16.1 %all_to_all.39.blocks_ref.old_blocks_ref = bf16[8,224,128]{2,1,0:T(8,128)(2,1)S(1)} all-to-all(bf16[8,224,128]{2,1,0:T(8,128)(2,1)S(1)} %bitcast.18), channel_id=1, replica_groups=mesh['layer'=2,'expert'=8,'row'=2] {'expert'}, dimensions={0} | all-to-all | bytes 917504 | tf_op jit(solution)/shard_map/all_to_all | solution.py:281
  54.5 0.0 copy-start.1
  54.5 3.1 %copy-done.1 = f32[224,64,128]{2,1,0:T(8,128)S(1)} copy-done((f32[224,64,128]{2,1,0:T(8,128)S(1)}, f32[224,64,128]{2,1,0:T(8,128)}, u32[]{:S(2)}) %copy-start.1) | copy-done | bytes 7340056
  57.6 2.8 %shard_map.75 = f32[16,8,64]{2,1,0:T(8,128)S(1)} custom-call(f32[224,64,128]{2,1,0:T(8,128)S(1)} %copy-done.1, bf16[8,224,128]{2,1,0:T(8,128)(2,1)S(1)} %all_to_all.39.blocks_ref.old_blocks_ref), custom_call_target="tpu_custom_call" | custom-call | flops 469762048 | bytes 7340032 | tf_op jit(solution)/shard_map/pallas_call | solution.py:110
  60.3 0.7 reshape.32
  61.1 3.6 %all-to-all-start.3 = ((f32[16,1,512]{2,1,0:T(1,128)}), f32[16,1,512]{2,1,0:T(1,128)S(1)}, u32[]{:S(2)}, u32[]{:S(2)}) async-start(f32[16,1,512]{2,1,0:T(1,128)} %reshape.32), calls=%async_computation.3 | async-start | bytes 65536 | tf_op jit(solution)/shard_map/all_to_all | solution.py:361
  64.7 0.0 copy-start.2
  64.7 3.1 %copy-done.2 = f32[224,64,128]{2,1,0:T(8,128)S(1)} copy-done((f32[224,64,128]{2,1,0:T(8,128)S(1)}, f32[224,64,128]{2,1,0:T(8,128)}, u32[]{:S(2)}) %copy-start.2) | copy-done | bytes 7340056
  67.7 3.8 %shard_map.76.bases_ref = bf16[224,64,128]{2,1,0:T(8,128)(2,1)S(1)} custom-call(f32[8,64]{1,0:T(8,128)S(1)} %bitcast.23, f32[224,64,128]{2,1,0:T(8,128)S(1)} %copy-done.2, bf16[8,224,128]{2,1,0:T(8,128)(2,1)S(1)} %all_to_all.39.blocks_ref.old_blocks_ref), custom_call_target="tpu_custom_call" | custom-call | flops 939524096 | bytes 14680064 | tf_op jit(solution)/shard_map/pallas_call | solution.py:110
  71.5 0.0 copy-start.7
  71.5 1.8 %copy-done.7 = bf16[224,64,128]{2,1,0:T(8,128)(2,1)} copy-done((bf16[224,64,128]{2,1,0:T(8,128)(2,1)}, bf16[224,64,128]{2,1,0:T(8,128)(2,1)S(1)}, u32[]{:S(2)}) %copy-start.7) | copy-done | bytes 3670040
  73.4 0.0 all-to-all-done.3
  73.4 0.6 broadcast.14
  74.0 0.7 reduce
  74.7 0.1 reshape.33.sums_ref
  74.8 0.0 copy-start.8
  74.8 2.0 %copy-done.8 = bf16[224,64,128]{2,1,0:T(8,128)(2,1)S(1)} copy-done((bf16[224,64,128]{2,1,0:T(8,128)(2,1)S(1)}, bf16[224,64,128]{2,1,0:T(8,128)(2,1)}, u32[]{:S(2)}) %copy-start.8) | copy-done | bytes 3670040
  76.8 4.8 %shard_map.77 = (bf16[8,224,128]{2,1,0:T(8,128)(2,1)}, f32[8,64]{1,0:T(8,128)S(1)}, f32[8,64]{1,0:T(8,128)S(1)}) custom-call(f32[16,8,64]{2,1,0:T(8,128)S(1)} %reshape.33.sums_ref, f32[8,64]{1,0:T(8,128)S(1)} %bitcast.24, bf16[224,64,128]{2,1,0:T(8,128)(2,1)S(1)} %copy-done.8), custom_call_target="tpu_custom_call" | custom-call | flops 939524096 | bytes 3670016 | tf_op jit(solution)/shard_map/pallas_call | solution.py:110
  81.7 5.9 %all-to-all-start.4 = ((bf16[8,224,128]{2,1,0:T(8,128)(2,1)}), bf16[8,224,128]{2,1,0:T(8,128)(2,1)S(1)}, u32[]{:S(2)}, u32[]{:S(2)}) async-start(bf16[8,224,128]{2,1,0:T(8,128)(2,1)} %get-tuple-element.18), calls=%async_computation.4 | async-start | bytes 917504 | tf_op jit(solution)/shard_map/all_to_all | solution.py:281
  87.6 0.0 copy-start.5
  87.6 2.0 %copy-done.5 = bf16[1,1024,1792]{2,1,0:T(8,128)(2,1)S(1)} copy-done((bf16[1,1024,1792]{2,1,0:T(8,128)(2,1)S(1)}, bf16[1,1024,1792]{2,1,0:T(8,128)(2,1)}, u32[]{:S(2)}) %copy-start.5) | copy-done | bytes 3670040
  89.6 1.5 %shard_map.72.mine_ref.mine_old_ref = bf16[1024,128]{1,0:T(8,128)(2,1)S(1)} custom-call(bf16[1024,1792]{1,0:T(8,128)(2,1)S(1)} %bitcast.11, bf16[1024,128]{1,0:T(8,128)(2,1)S(1)} %get-tuple-element.13.low_ref, bf16[1792,128]{1,0:T(8,128)(2,1)S(1)} %bitcast.15), custom_call_target="tpu_custom_call" | custom-call | flops 469762048 | bytes 4128768 | tf_op jit(solution)/shard_map/pallas_call | solution.py:110
  91.2 0.1 collective-permute-start.1
  91.2 1.5 %collective-permute-done.1.other_ref.other_old_ref = bf16[1024,128]{1,0:T(8,128)(2,1)S(1)} collective-permute-done((bf16[1024,128]{1,0:T(8,128)(2,1)S(1)}, bf16[1024,128]{1,0:T(8,128)(2,1)S(1)}, u32[]{:S(2)}, u32[]{:S(2)}) %collective-permute-start.1) | collective-permute-done | bytes 262176 | tf_op jit(solution)/shard_map/ppermute | solution.py:277
  92.8 1.0 copy-done.12
  93.8 0.9 shard_map.73
  94.7 6.3 %all-to-all-done.4 = bf16[8,224,128]{2,1,0:T(8,128)(2,1)S(1)} async-done(((bf16[8,224,128]{2,1,0:T(8,128)(2,1)}), bf16[8,224,128]{2,1,0:T(8,128)(2,1)S(1)}, u32[]{:S(2)}, u32[]{:S(2)}) %all-to-all-start.4) | async-done | bytes 458784 | tf_op jit(solution)/shard_map/all_to_all | solution.py:281
  101.0 1.2 shard_map.80
  102.1 3.6 %all-to-all-start.5 = ((bf16[8,224,128]{2,1,0:T(8,128)(2,1)}), bf16[8,224,128]{2,1,0:T(8,128)(2,1)S(1)}, u32[]{:S(2)}, u32[]{:S(2)}) async-start(bf16[8,224,128]{2,1,0:T(8,128)(2,1)} %bitcast.9), calls=%async_computation.5 | async-start | bytes 917504 | tf_op jit(solution)/shard_map/all_to_all | solution.py:281
  105.8 2.0 %copy-done.6 = bf16[1,1024,1792]{2,1,0:T(8,128)(2,1)S(1)} copy-done((bf16[1,1024,1792]{2,1,0:T(8,128)(2,1)S(1)}, bf16[1,1024,1792]{2,1,0:T(8,128)(2,1)}, u32[]{:S(2)}) %copy-start.6) | copy-done | bytes 3670040
  107.8 1.5 %shard_map.78.mine_ref = bf16[1024,128]{1,0:T(8,128)(2,1)S(1)} custom-call(bf16[1024,1792]{1,0:T(8,128)(2,1)S(1)} %bitcast.13, bf16[1024,128]{1,0:T(8,128)(2,1)S(1)} %get-tuple-element.15.low_ref, bf16[1792,128]{1,0:T(8,128)(2,1)S(1)} %bitcast.17), custom_call_target="tpu_custom_call" | custom-call | flops 469762048 | bytes 4128768 | tf_op jit(solution)/shard_map/pallas_call | solution.py:110
  109.3 0.1 collective-permute-start.2
  109.4 1.5 %collective-permute-done.2.other_ref = bf16[1024,128]{1,0:T(8,128)(2,1)S(1)} collective-permute-done((bf16[1024,128]{1,0:T(8,128)(2,1)S(1)}, bf16[1024,128]{1,0:T(8,128)(2,1)S(1)}, u32[]{:S(2)}, u32[]{:S(2)}) %collective-permute-start.2) | collective-permute-done | bytes 262176 | tf_op jit(solution)/shard_map/ppermute | solution.py:277
  110.9 1.0 shard_map.79
  111.9 7.1 %all-to-all-done.5.blocks_ref = bf16[8,224,128]{2,1,0:T(8,128)(2,1)S(1)} async-done(((bf16[8,224,128]{2,1,0:T(8,128)(2,1)}), bf16[8,224,128]{2,1,0:T(8,128)(2,1)S(1)}, u32[]{:S(2)}, u32[]{:S(2)}) %all-to-all-start.5) | async-done | bytes 458784 | tf_op jit(solution)/shard_map/all_to_all | solution.py:281
  119.0 2.0 %copy-done.9 = bf16[224,64,128]{2,1,0:T(8,128)(2,1)S(1)} copy-done((bf16[224,64,128]{2,1,0:T(8,128)(2,1)S(1)}, bf16[224,64,128]{2,1,0:T(8,128)(2,1)}, u32[]{:S(2)}) %copy-start.9) | copy-done | bytes 3670040
  121.1 2.8 %shard_map.82 = f32[16,8,64]{2,1,0:T(8,128)S(1)} custom-call(bf16[224,64,128]{2,1,0:T(8,128)(2,1)S(1)} %copy-done.9, bf16[8,224,128]{2,1,0:T(8,128)(2,1)S(1)} %all-to-all-done.5.blocks_ref), custom_call_target="tpu_custom_call" | custom-call | flops 469762048 | bytes 3670016 | tf_op jit(solution)/shard_map/pallas_call | solution.py:110
  123.8 0.7 reshape.34
  124.6 3.7 %all-to-all-start.6 = ((f32[16,1,512]{2,1,0:T(1,128)}), f32[16,1,512]{2,1,0:T(1,128)S(1)}, u32[]{:S(2)}, u32[]{:S(2)}) async-start(f32[16,1,512]{2,1,0:T(1,128)} %reshape.34), calls=%async_computation.6 | async-start | bytes 65536 | tf_op jit(solution)/shard_map/all_to_all | solution.py:386
  128.3 0.0 copy-start.3
  128.3 3.1 %copy-done.3 = f32[224,64,128]{2,1,0:T(8,128)S(1)} copy-done((f32[224,64,128]{2,1,0:T(8,128)S(1)}, f32[224,64,128]{2,1,0:T(8,128)}, u32[]{:S(2)}) %copy-start.3) | copy-done | bytes 7340056
  131.4 9.4 %shard_map.81 = f32[224,64,128]{2,1,0:T(8,128)} custom-call(f32[8,64]{1,0:T(8,128)S(1)} %bitcast.25, f32[8,64]{1,0:T(8,128)S(1)} %get-tuple-element.19.new_ref, f32[224,64,128]{2,1,0:T(8,128)S(1)} %copy-done.3, bf16[8,224,128]{2,1,0:T(8,128)(2,1)S(1)} %all_to_all.39.blocks_ref.old_blocks_ref, bf16[8,224,128]{2,1,0:T(8,128)(2,1)S(1)} %all-to-all-done.5.blocks_ref), custom_call_target="tpu_custom_call" | custom-call | flops 1879048192 | bytes 14680064 | tf_op jit(solution)/shard_map/pallas_call | solution.py:110
  140.8 0.0 all-to-all-done.6
  140.8 0.8 reduce.1
  141.6 0.1 reshape.35
  141.7 0.0 copy-done.13
  141.7 0.5 divide_subtract_fusion
  (5 shorter events, 0.0 us)
Async XLA Ops:
  14.8 3.1 %copy-start = (f32[224,64,128]{2,1,0:T(8,128)S(1)}, f32[224,64,128]{2,1,0:T(8,128)}, u32[]{:S(2)}) copy-start(f32[224,64,128]{2,1,0:T(8,128)} %bases_ref.7) | copy-start | bytes 22020100
  17.9 8.3 %copy-start.10 = (f32[1,512,128]{2,1,0:T(8,128)S(1)}, f32[1,512,128]{2,1,0:T(8,128)}, u32[]{:S(2)}) copy-start(f32[1,512,128]{2,1,0:T(8,128)} %param.5) | copy-start | bytes 786436
  22.7 15.3 %all-to-all-start.1 = ((bf16[8,224,128]{2,1,0:T(8,128)(2,1)}), bf16[8,224,128]{2,1,0:T(8,128)(2,1)S(1)}, u32[]{:S(2)}, u32[]{:S(2)}) async-start(bf16[8,224,128]{2,1,0:T(8,128)(2,1)} %shard_map.71), calls=%async_computation.1 | async-start | bytes 917504 | tf_op jit(solution)/shard_map/all_to_all | solution.py:281
  26.1 1.6 %collective-permute-start = (f32[512,128]{1,0:T(8,128)S(1)}, f32[512,128]{1,0:T(8,128)S(1)}, u32[]{:S(2)}, u32[]{:S(2)}) collective-permute-start(f32[512,128]{1,0:T(8,128)S(1)} %bitcast.19), channel_id=1, source_target_pairs={{0,1},{1,0},{2,3},{3,2},{4,5},{5,4},{6,7},{7,6},{8,9},{9,8},{10,11... | collective-permute-start | bytes 786440 | tf_op jit(solution)/shard_map/ppermute | solution.py:277
  27.8 2.0 %copy-start.4 = (bf16[1,1024,1792]{2,1,0:T(8,128)(2,1)S(1)}, bf16[1,1024,1792]{2,1,0:T(8,128)(2,1)}, u32[]{:S(2)}) copy-start(bf16[1,1024,1792]{2,1,0:T(8,128)(2,1)} %param.4) | copy-start | bytes 11010052
  30.7 0.8 copy-start.11
  54.5 3.1 %copy-start.1 = (f32[224,64,128]{2,1,0:T(8,128)S(1)}, f32[224,64,128]{2,1,0:T(8,128)}, u32[]{:S(2)}) copy-start(f32[224,64,128]{2,1,0:T(8,128)} %bases_ref.7) | copy-start | bytes 22020100
  61.1 12.3 %all-to-all-start.3 = ((f32[16,1,512]{2,1,0:T(1,128)}), f32[16,1,512]{2,1,0:T(1,128)S(1)}, u32[]{:S(2)}, u32[]{:S(2)}) async-start(f32[16,1,512]{2,1,0:T(1,128)} %reshape.32), calls=%async_computation.3 | async-start | bytes 65536 | tf_op jit(solution)/shard_map/all_to_all | solution.py:361
  64.7 3.1 %copy-start.2 = (f32[224,64,128]{2,1,0:T(8,128)S(1)}, f32[224,64,128]{2,1,0:T(8,128)}, u32[]{:S(2)}) copy-start(f32[224,64,128]{2,1,0:T(8,128)} %bases_ref.7) | copy-start | bytes 22020100
  71.5 1.8 %copy-start.7 = (bf16[224,64,128]{2,1,0:T(8,128)(2,1)}, bf16[224,64,128]{2,1,0:T(8,128)(2,1)S(1)}, u32[]{:S(2)}) copy-start(bf16[224,64,128]{2,1,0:T(8,128)(2,1)S(1)} %shard_map.76.bases_ref) | copy-start | bytes 11010052
  74.8 2.0 %copy-start.8 = (bf16[224,64,128]{2,1,0:T(8,128)(2,1)S(1)}, bf16[224,64,128]{2,1,0:T(8,128)(2,1)}, u32[]{:S(2)}) copy-start(bf16[224,64,128]{2,1,0:T(8,128)(2,1)} %copy-done.7) | copy-start | bytes 11010052
  81.7 19.3 %all-to-all-start.4 = ((bf16[8,224,128]{2,1,0:T(8,128)(2,1)}), bf16[8,224,128]{2,1,0:T(8,128)(2,1)S(1)}, u32[]{:S(2)}, u32[]{:S(2)}) async-start(bf16[8,224,128]{2,1,0:T(8,128)(2,1)} %get-tuple-element.18), calls=%async_computation.4 | async-start | bytes 917504 | tf_op jit(solution)/shard_map/all_to_all | solution.py:281
  87.6 2.0 %copy-start.5 = (bf16[1,1024,1792]{2,1,0:T(8,128)(2,1)S(1)}, bf16[1,1024,1792]{2,1,0:T(8,128)(2,1)}, u32[]{:S(2)}) copy-start(bf16[1,1024,1792]{2,1,0:T(8,128)(2,1)} %param.4) | copy-start | bytes 11010052
  91.2 1.6 %collective-permute-start.1 = (bf16[1024,128]{1,0:T(8,128)(2,1)S(1)}, bf16[1024,128]{1,0:T(8,128)(2,1)S(1)}, u32[]{:S(2)}, u32[]{:S(2)}) collective-permute-start(bf16[1024,128]{1,0:T(8,128)(2,1)S(1)} %shard_map.72.mine_ref.mine_old_ref), channel_id=1, source_target_pairs={{0,1},{1,0},{2,3},{3,2},{4,5},{5,4},{6,7},{7,6},{8,9},{9,8},{10,11... | collective-permute-start | bytes 786440 | tf_op jit(solution)/shard_map/ppermute | solution.py:277
  92.8 1.0 copy-start.12
  102.1 16.9 %all-to-all-start.5 = ((bf16[8,224,128]{2,1,0:T(8,128)(2,1)}), bf16[8,224,128]{2,1,0:T(8,128)(2,1)S(1)}, u32[]{:S(2)}, u32[]{:S(2)}) async-start(bf16[8,224,128]{2,1,0:T(8,128)(2,1)} %bitcast.9), calls=%async_computation.5 | async-start | bytes 917504 | tf_op jit(solution)/shard_map/all_to_all | solution.py:281
  105.8 2.0 %copy-start.6 = (bf16[1,1024,1792]{2,1,0:T(8,128)(2,1)S(1)}, bf16[1,1024,1792]{2,1,0:T(8,128)(2,1)}, u32[]{:S(2)}) copy-start(bf16[1,1024,1792]{2,1,0:T(8,128)(2,1)} %param.4) | copy-start | bytes 11010052
  109.3 1.6 %collective-permute-start.2 = (bf16[1024,128]{1,0:T(8,128)(2,1)S(1)}, bf16[1024,128]{1,0:T(8,128)(2,1)S(1)}, u32[]{:S(2)}, u32[]{:S(2)}) collective-permute-start(bf16[1024,128]{1,0:T(8,128)(2,1)S(1)} %shard_map.78.mine_ref), channel_id=1, source_target_pairs={{0,1},{1,0},{2,3},{3,2},{4,5},{5,4},{6,7},{7,6},{8,9},{9,8},{10,11... | collective-permute-start | bytes 786440 | tf_op jit(solution)/shard_map/ppermute | solution.py:277
  119.0 2.0 %copy-start.9 = (bf16[224,64,128]{2,1,0:T(8,128)(2,1)S(1)}, bf16[224,64,128]{2,1,0:T(8,128)(2,1)}, u32[]{:S(2)}) copy-start(bf16[224,64,128]{2,1,0:T(8,128)(2,1)} %copy-done.7) | copy-start | bytes 11010052
  124.6 16.3 %all-to-all-start.6 = ((f32[16,1,512]{2,1,0:T(1,128)}), f32[16,1,512]{2,1,0:T(1,128)S(1)}, u32[]{:S(2)}, u32[]{:S(2)}) async-start(f32[16,1,512]{2,1,0:T(1,128)} %reshape.34), calls=%async_computation.6 | async-start | bytes 65536 | tf_op jit(solution)/shard_map/all_to_all | solution.py:386
  128.3 3.1 %copy-start.3 = (f32[224,64,128]{2,1,0:T(8,128)S(1)}, f32[224,64,128]{2,1,0:T(8,128)}, u32[]{:S(2)}) copy-start(f32[224,64,128]{2,1,0:T(8,128)} %bases_ref.7) | copy-start | bytes 22020100
  131.4 10.3 %copy-start.13 = (f32[1,64]{1,0:T(1,128)S(1)}, f32[1,64]{1,0:T(1,128)}, u32[]{:S(2)}) copy-start(f32[1,64]{1,0:T(1,128)} %param.6) | copy-start | bytes 772

commit v2 on v1

v2 whole, which is shorter than its diff:
```python
import functools
import math

import jax
import jax.numpy as jnp
from jax import lax
from jax.experimental import pallas as pl
from jax.experimental.pallas import tpu as pltpu
from jax.sharding import PartitionSpec as P

ITERS = 2


BETA_ONE = 0.9
BETA_TWO = 0.999
RATE = 0.3
EPSILON_FACTORS = 8.0
EPSILON_BASES = 6.0
EPSILON_MIXING = 300.0

FIRST_OLD = BETA_ONE * (1.0 - BETA_ONE) / (1.0 - BETA_ONE**2)
FIRST_NEW = (1.0 - BETA_ONE) / (1.0 - BETA_ONE**2)
SECOND_OLD = BETA_TWO * (1.0 - BETA_TWO) / (1.0 - BETA_TWO**2)
SECOND_NEW = (1.0 - BETA_TWO) / (1.0 - BETA_TWO**2)

GROUP = 16
CHUNK = 32
MEGABYTE = 1 << 20
TINY = 1e-30
TAIL = 16


def adam_update(values, moment_one, moment_two, gradient, iteration, epsilon):
    moment_one = BETA_ONE * moment_one + (1.0 - BETA_ONE) * gradient
    moment_two = BETA_TWO * moment_two + (1.0 - BETA_TWO) * gradient * gradient
    correct_one = 1.0 - BETA_ONE**iteration
    correct_two = 1.0 - BETA_TWO**iteration
    values = values - RATE * (moment_one / correct_one) / (
        jnp.sqrt(moment_two / correct_two) + epsilon
    )
    return (values, moment_one, moment_two)


def ratio(top, bottom):
    guess = pltpu.reciprocal(bottom, approx=True)
    return top * (guess * (2.0 - bottom * guess))


def first_step(values, gradient, epsilon):
    return values - ratio(RATE * gradient, jnp.abs(gradient) + epsilon)


def last_step(values, old, new, epsilon):
    top = (RATE * FIRST_OLD) * old + (RATE * FIRST_NEW) * new
    square = SECOND_OLD * (old * old) + SECOND_NEW * (new * new)
    return values - ratio(top, square * lax.rsqrt(square + TINY) + epsilon)


def second_step(values, old, new, epsilon):
    return last_step(first_step(values, old, epsilon), old, new, epsilon)


def halves(array):
    high = array.astype(jnp.bfloat16)
    low = (array - high.astype(jnp.float32)).astype(jnp.bfloat16)
    return (high, low)


def dot(left, right, contract=((1,), (0,))):
    return lax.dot_general(left, right, (contract, ((), ())), preferred_element_type=jnp.float32)


def spread_rows(mixing, scale):
    experts, bases = mixing.shape
    rows, columns = experts * GROUP, GROUP * bases
    pick = (
        (lax.broadcasted_iota(jnp.int32, (rows, experts), 0) >> 4)
        == lax.broadcasted_iota(jnp.int32, (rows, experts), 1)
    ).astype(jnp.bfloat16)
    tile = (
        lax.broadcasted_iota(jnp.int32, (bases, columns), 0)
        == (lax.broadcasted_iota(jnp.int32, (bases, columns), 1) & 63)
    ).astype(jnp.bfloat16)
    keep = (
        (lax.broadcasted_iota(jnp.int32, (rows, columns), 0) & 15)
        == (lax.broadcasted_iota(jnp.int32, (rows, columns), 1) >> 6)
    )
    parts = []
    for half in halves(scale * mixing):
        wide = dot(half, tile).astype(jnp.bfloat16)
        parts.append(jnp.where(keep, dot(pick, wide), 0.0).astype(jnp.bfloat16))
    return jnp.concatenate(parts, axis=0)


def spread_columns(mixing, scale):
    experts, bases = mixing.shape
    rows, columns = GROUP * bases, experts * GROUP
    pick = (
        lax.broadcasted_iota(jnp.int32, (experts, columns), 0)
        == (lax.broadcasted_iota(jnp.int32, (experts, columns), 1) >> 4)
    ).astype(jnp.bfloat16)
    tile = (
        (lax.broadcasted_iota(jnp.int32, (rows, bases), 0) & 63)
        == lax.broadcasted_iota(jnp.int32, (rows, bases), 1)
    ).astype(jnp.bfloat16)
    keep = (
        (lax.broadcasted_iota(jnp.int32, (rows, columns), 0) >> 6)
        == (lax.broadcasted_iota(jnp.int32, (rows, columns), 1) & 15)
    )
    parts = []
    for half in halves(scale * mixing):
        wide = dot(half, pick, ((0,), (0,))).astype(jnp.bfloat16)
        parts.append(jnp.where(keep, dot(tile, wide), 0.0).astype(jnp.bfloat16))
    return jnp.concatenate(parts, axis=1)


def far_memory(specs):
    return specs is not None and any(spec.memory_space == pltpu.HBM for spec in specs)


def call(kernel, out_shape, *args, grid=(), in_specs=None, out_specs=None, scratch=(), flops=0, traffic=0, limit=24):
    whole = pl.BlockSpec(memory_space=pltpu.VMEM)
    single = isinstance(out_shape, jax.ShapeDtypeStruct)
    return pl.pallas_call(
        kernel,
        out_shape=out_shape,
        grid=grid,
        in_specs=[whole] * len(args) if in_specs is None else in_specs,
        out_specs=(whole if single else [whole] * len(out_shape)) if out_specs is None else out_specs,
        scratch_shapes=list(scratch),
        compiler_params=pltpu.CompilerParams(vmem_limit_bytes=(61 if far_memory(in_specs) else limit) * MEGABYTE),
        cost_estimate=pl.CostEstimate(flops=flops, bytes_accessed=traffic, transcendentals=0),
    )(*args)


def shape_of(shape, dtype):
    return jax.ShapeDtypeStruct(tuple(shape), dtype)


def store_products(weights_ref, low, product_ref, gram_ref):
    product_ref[...] = dot(low, weights_ref[...], ((0,), (0,))).T
    gram_ref[...] = dot(low, low, ((0,), (0,)))


def start_kernel(
    row_ref, far_weights_ref, own_ref, other_ref, mixing_ref, full_ref, low_ref, out_ref, weights_ref, sem
):
    load = pltpu.make_async_copy(far_weights_ref, weights_ref, sem)
    load.start()
    rows = own_ref.shape[0]
    row = row_ref[0]
    full_ref[pl.ds(pl.multiple_of(row * rows, rows), rows), :] = own_ref[...]
    full_ref[pl.ds(pl.multiple_of((1 - row) * rows, rows), rows), :] = other_ref[...]
    low = full_ref[...].astype(jnp.bfloat16)
    low_ref[...] = low
    experts, height, rank = out_ref.shape
    columns = height - rank - TAIL
    gram = dot(low, low, ((0,), (0,)))
    high = gram.astype(jnp.bfloat16)
    out_ref[:, columns : columns + rank, :] = jnp.broadcast_to(high[None], (experts, rank, rank))
    diagonal = lax.broadcasted_iota(jnp.int32, gram.shape, 0) == lax.broadcasted_iota(jnp.int32, gram.shape, 1)
    rest = jnp.sum(jnp.where(diagonal, gram - high.astype(jnp.float32), 0.0), axis=0, keepdims=True)
    mixing = mixing_ref[...]
    mixing = jnp.concatenate([mixing, jnp.zeros((1, rank - mixing.shape[1]), jnp.float32)], axis=1)
    first = mixing.astype(jnp.bfloat16).astype(jnp.float32)
    second = (mixing - first).astype(jnp.bfloat16).astype(jnp.float32)
    third = mixing - first - second
    place = lax.broadcasted_iota(jnp.int32, (TAIL, rank), 0)
    tail = jnp.zeros((TAIL, rank), jnp.float32)
    for position, part in enumerate((first, second, third, rest)):
        tail = jnp.where(place == position, part, tail)
    out_ref[:, columns + rank :, :] = jnp.broadcast_to(tail.astype(jnp.bfloat16)[None], (experts, TAIL, rank))
    load.wait()
    product = dot(low, weights_ref[...], ((0,), (0,))).T.astype(jnp.bfloat16)
    out_ref[:, :columns, :] = product.reshape(experts, columns, rank)


def step_kernel(weights_ref, full_ref, mine_ref, other_ref, low_ref, product_ref, gram_ref):
    gradient = mine_ref[...] + other_ref[...]
    low = first_step(full_ref[...], gradient, EPSILON_FACTORS).astype(jnp.bfloat16)
    low_ref[...] = low
    store_products(weights_ref, low, product_ref, gram_ref)


def panel_kernel(panels_ref, product_ref, gram_ref, out_ref):
    high, low = halves(gram_ref[...])
    panels = panels_ref[...]
    out_ref[...] = (dot(panels, high) + dot(panels, low) - product_ref[...]).astype(jnp.bfloat16)


def factor_kernel(weights_ref, low_ref, panels_ref, out_ref):
    experts, _, rank = panels_ref.shape
    columns = weights_ref.shape[1] // experts
    panels = panels_ref[:, :columns, :].reshape(-1, rank)
    high, low = halves(dot(panels, panels, ((0,), (0,))))
    factors = low_ref[...]
    out_ref[...] = dot(factors, high) + dot(factors, low) - dot(weights_ref[...], panels)


def last_factor_kernel(row_ref, own_ref, mine_old_ref, other_old_ref, mine_ref, other_ref, out_ref):
    rows = own_ref.shape[0]
    here = pl.ds(pl.multiple_of(row_ref[0] * rows, rows), rows)
    old = mine_old_ref[here, :] + other_old_ref[here, :]
    new = mine_ref[here, :] + other_ref[here, :]
    out_ref[...] = second_step(own_ref[...], old, new, EPSILON_FACTORS)


def pair_of(ref, pair):
    start = pl.multiple_of(pair * 2 * GROUP, 2 * GROUP)
    parts = [ref[pl.ds(start + half * GROUP, GROUP)] for half in range(2)]
    return [part.reshape(-1, part.shape[-1]) for part in parts]


def blocks_of(ref, pair):
    start = pl.multiple_of(pair * 2 * GROUP, 2 * GROUP)
    parts = [ref[:, pl.ds(start + half * GROUP, GROUP), :] for half in range(2)]
    return jnp.concatenate([part.reshape(-1, part.shape[-1]) for part in parts], axis=1)


def put_pair(ref, pair, wide):
    rank = wide.shape[1] // 2
    start = pl.multiple_of(pair * 2 * GROUP, 2 * GROUP)
    for half in range(2):
        part = wide[:, half * rank : (half + 1) * rank].astype(ref.dtype)
        ref[pl.ds(start + half * GROUP, GROUP)] = part.reshape(GROUP, -1, rank)


def copy_of(source, target, sems, pair):
    part = pl.ds(pl.multiple_of(pair * CHUNK, CHUNK), CHUNK)
    return pltpu.make_async_copy(source.at[part], target.at[part], sems.at[pair])


def each_pair(columns, step):
    lax.fori_loop(0, columns // CHUNK, lambda pair, _: step(pair), None)


def start_copies(source, target, sems):
    each_pair(source.shape[0], lambda pair: copy_of(source, target, sems, pair).start())


def wait_copies(source, target, sems):
    each_pair(source.shape[0], lambda pair: copy_of(source, target, sems, pair).wait())


def run_pairs(source, target, sems, step, batch=3):
    count = source.shape[0] // CHUNK
    for first in range(0, count, batch):
        batch_pairs = range(first, min(first + batch, count))
        for pair in batch_pairs:
            copy_of(source, target, sems, pair).wait()
        for pair in batch_pairs:
            step(pair)


def low_pair(ref, pair):
    return jnp.concatenate([part.astype(jnp.bfloat16) for part in pair_of(ref, pair)], axis=1)


def low_rest_pair(ref, pair):
    parts = [halves(part) for part in pair_of(ref, pair)]
    return [jnp.concatenate(side, axis=1) for side in zip(*parts)]


def mix_groups(spread, bases_ref, bases, sems, out_ref):
    half = spread.shape[0] // 2
    rank = bases.shape[-1]

    def step(pair):
        if bases.dtype == jnp.float32:
            high, low = low_rest_pair(bases, pair)
            both = dot(spread[...], high)
            mixed = both[:half] + both[half:] + dot(spread[:half], low)
        else:
            both = dot(spread[...], low_pair(bases, pair))
            mixed = both[:half] + both[half:]
        mixed = mixed.astype(jnp.bfloat16)
        start = pair * CHUNK
        for part in range(2):
            out_ref[:, pl.ds(start + part * GROUP, GROUP), :] = mixed[:, part * rank : (part + 1) * rank].reshape(
                -1, GROUP, rank
            )

    run_pairs(bases_ref, bases, sems, step)


def fold_total(scale, total, lanes):
    rows, columns = total.shape
    experts = rows // GROUP
    keep = (lax.broadcasted_iota(jnp.int32, (rows, columns), 0) & 15) == (
        lax.broadcasted_iota(jnp.int32, (rows, columns), 1) >> 6
    )
    wide = jnp.where(keep, total[...], 0.0).reshape(experts, GROUP, columns).sum(axis=1)
    fold = (
        (lax.broadcasted_iota(jnp.int32, (columns, lanes), 0) & 63)
        == lax.broadcasted_iota(jnp.int32, (columns, lanes), 1)
    ).astype(jnp.float32)
    return scale * lax.dot_general(
        wide, fold, (((1,), (0,)), ((), ())),
        precision=lax.Precision.HIGHEST, preferred_element_type=jnp.float32,
    )


def first_kernel(scale, sent_ref, bases_ref, out_ref, blocks_ref, mixing_ref, spread, total, blocks_rest, bases, sems):
    start_copies(bases_ref, bases, sems)
    columns, count, rank = bases.shape
    experts = sent_ref.shape[0]
    tail = sent_ref[:, columns + rank :, :].astype(jnp.float32)
    place = lax.broadcasted_iota(jnp.int32, tail.shape, 1)
    mixing = jnp.sum(jnp.where(place < 3, tail, 0.0), axis=1)[:, :count]
    rest = jnp.sum(jnp.where(place == 3, tail, 0.0), axis=1)
    mixing_ref[...] = mixing
    spread[...] = spread_rows(mixing, scale)
    mix_groups(spread, bases_ref, bases, sems, out_ref)
    for expert in range(experts):
        mixed = out_ref[expert, :columns, :]
        blocks_ref[expert], blocks_rest[expert] = halves(
            dot(mixed, sent_ref[expert, columns : columns + rank, :])
            + mixed.astype(jnp.float32) * rest[expert : expert + 1]
            - sent_ref[expert, :columns, :].astype(jnp.float32)
        )
    half = total.shape[0]
    result = None
    for pair in range(columns // CHUNK):
        high, low = low_rest_pair(bases, pair)
        blocks = blocks_of(blocks_ref, pair)
        both = dot(jnp.concatenate([blocks, blocks_of(blocks_rest, pair)], axis=0), high, ((1,), (1,)))
        product = both[:half] + both[half:] + dot(blocks, low, ((1,), (1,)))
        result = product if result is None else result + product
    total[...] = result
    high, low = halves(fold_total(scale, total, rank))
    sums = jnp.concatenate([high, low], axis=0)
    out_ref[:, columns:, :] = jnp.broadcast_to(sums[None], (experts,) + sums.shape)


def sum_kernel(sent_ref, out_ref):
    experts, rank = out_ref.shape
    start = sent_ref.shape[1] - 2 * experts
    sums = jnp.sum(sent_ref[:, start:, :].astype(jnp.float32), axis=0)
    out_ref[...] = sums[:experts] + sums[experts:]


def next_mix_kernel(scale, mine_ref, other_ref, mixing_ref, bases_ref, out_ref, next_ref, grad_ref, spread, bases, sems):
    start_copies(bases_ref, bases, sems)
    mixing = mixing_ref[...]
    gradient = (mine_ref[...] + other_ref[...])[:, : mixing.shape[1]]
    following = first_step(mixing, gradient, EPSILON_MIXING)
    next_ref[...] = following
    grad_ref[...] = gradient
    spread[...] = spread_rows(following, scale)
    mix_groups(spread, bases_ref, bases, sems, out_ref)


def mixing_kernel(scale, bases_ref, blocks_ref, out_ref, total, bases, sems):
    start_copies(bases_ref, bases, sems)
    total[...] = jnp.zeros_like(total)

    def step(pair):
        total[...] += dot(blocks_of(blocks_ref, pair), low_pair(bases, pair), ((1,), (1,)))

    run_pairs(bases_ref, bases, sems, step)
    gradient = fold_total(scale, total, out_ref.shape[-1])
    out_ref[...] = jnp.broadcast_to(gradient[None], out_ref.shape)


def gradient_pair(spread, blocks_ref, pair):
    blocks = blocks_of(blocks_ref, pair)
    return dot(spread[...], jnp.concatenate([blocks, blocks], axis=0))


def base_kernel(scale, mixing_ref, bases_ref, blocks_ref, out_ref, spread, bases, result, sems, out_sems):
    start_copies(bases_ref, bases, sems)
    spread[...] = spread_columns(mixing_ref[...], scale)

    def step(pair):
        gradient = gradient_pair(spread, blocks_ref, pair)
        copy_of(bases_ref, bases, sems, pair).wait()
        values = jnp.concatenate(pair_of(bases, pair), axis=1)
        put_pair(result, pair, first_step(values, gradient, EPSILON_BASES))
        copy_of(result, out_ref, out_sems, pair).start()

    each_pair(bases.shape[0], step)
    wait_copies(result, out_ref, out_sems)


def last_base_kernel(
    scale, old_ref, new_ref, bases_ref, old_blocks_ref, blocks_ref, out_ref,
    old_spread, spread, bases, sems, out_sems,
):
    start_copies(bases_ref, bases, sems)
    old_scale, new_scale = math.sqrt(SECOND_OLD), math.sqrt(SECOND_NEW)
    old_spread[...] = spread_columns(old_ref[...], scale * old_scale)
    spread[...] = spread_columns(new_ref[...], scale * new_scale)

    def step(pair):
        old = gradient_pair(old_spread, old_blocks_ref, pair)
        new = gradient_pair(spread, blocks_ref, pair)
        copy_of(bases_ref, bases, sems, pair).wait()
        values = jnp.concatenate(pair_of(bases, pair), axis=1)
        top = (RATE * FIRST_OLD / old_scale) * old + (RATE * FIRST_NEW / new_scale) * new
        square = old * old + new * new
        put_pair(bases, pair, values - ratio(top, square * lax.rsqrt(square + TINY) + EPSILON_BASES))
        copy_of(bases, out_ref, out_sems, pair).start()

    each_pair(bases.shape[0], step)
    wait_copies(bases, out_ref, out_sems)


def last_mixing_kernel(expert_ref, mixing_ref, old_ref, sums_ref, out_ref):
    experts, bases = old_ref.shape
    mine = lax.broadcasted_iota(jnp.int32, (experts, bases), 0) == expert_ref[0]
    new = jnp.sum(sums_ref[...], axis=0)[:, :bases]
    old = jnp.sum(jnp.where(mine, old_ref[...], 0.0), axis=0, keepdims=True)
    new = jnp.sum(jnp.where(mine, new, 0.0), axis=0, keepdims=True)
    out_ref[...] = second_step(mixing_ref[...], old, new, EPSILON_MIXING)


def swap_rows(array):
    return lax.ppermute(array, "row", [(0, 1), (1, 0)])


def exchange(array):
    return lax.all_to_all(array, "expert", split_axis=0, concat_axis=0, tiled=True)


def kernel_body(weights, factors, mixing, shared_bases):
    bf16, f32 = jnp.bfloat16, jnp.float32
    weights = weights[0]
    factors = factors[0]
    height, width = weights.shape
    own_rows, rank = factors.shape
    columns, bases, _ = shared_bases.shape
    experts = width // columns
    devices = experts * (height // own_rows)
    scale = 1.0 / math.sqrt(bases * rank)
    row = lax.axis_index("row").reshape(1)
    expert = lax.axis_index("expert").reshape(1)
    scalar = pl.BlockSpec(memory_space=pltpu.SMEM)
    whole = pl.BlockSpec(memory_space=pltpu.VMEM)

    wide_flops = 2 * height * width * rank
    mix_flops = 2 * columns * GROUP * experts * bases * rank
    block_bytes = 2 * width * rank
    base_bytes = 4 * shared_bases.size

    far = pl.BlockSpec(memory_space=pltpu.HBM)
    sems = pltpu.SemaphoreType.DMA((columns // CHUNK,))
    wide_scratch = pltpu.VMEM(shared_bases.shape, f32)
    thin_scratch = pltpu.VMEM(shared_bases.shape, bf16)
    blocks = shape_of((experts, columns, rank), bf16)
    panels_shape = shape_of((width, rank), bf16)
    small = shape_of((experts, bases), f32)
    rows_spread = pltpu.VMEM((2 * experts * GROUP, GROUP * bases), bf16)
    columns_spread = pltpu.VMEM((GROUP * bases, 2 * experts * GROUP), bf16)
    products = [shape_of((height, rank), bf16), shape_of((width, rank), f32), shape_of((rank, rank), f32)]

    def factor_part(low, panels):
        return call(
            factor_kernel, shape_of((height, rank), f32), weights, low, panels,
            flops=wide_flops, traffic=weights.size * 2 + block_bytes,
        )

    def panel_part(panels, product, gram):
        return call(
            panel_kernel, panels_shape, panels, product, gram, flops=wide_flops // 8, traffic=4 * block_bytes
        ).reshape(blocks.shape)

    def mixing_part(values, collected):
        return call(
            functools.partial(mixing_kernel, scale),
            shape_of((devices, experts, rank), f32), values, collected,
            in_specs=[far, whole],
            scratch=[
                pltpu.VMEM((experts * GROUP, GROUP * bases), f32), pltpu.VMEM(values.shape, values.dtype), sems
            ],
            flops=mix_flops, traffic=values.size * values.dtype.itemsize,
        )

    full, low_one, sent = call(
        start_kernel,
        [shape_of((height, rank), f32), products[0], shape_of((experts, columns + rank + TAIL, rank), bf16)],
        row, weights, factors, swap_rows(factors), mixing,
        in_specs=[scalar, far] + [whole] * 3,
        scratch=[pltpu.VMEM(weights.shape, bf16), pltpu.SemaphoreType.DMA(())],
        flops=wide_flops, traffic=weights.size * 2 + 4 * block_bytes,
    )

    sent = exchange(sent)
    mixed_one, collected_one, mixing_all = call(
        functools.partial(first_kernel, scale),
        [shape_of((experts, columns + 2 * experts, rank), bf16), blocks, small], sent, shared_bases,
        in_specs=[whole, far],
        scratch=[
            rows_spread, pltpu.VMEM((experts * GROUP, GROUP * bases), f32), pltpu.VMEM(blocks.shape, bf16),
            wide_scratch, sems,
        ],
        flops=3 * mix_flops, traffic=base_bytes,
    )
    panels_one = exchange(mixed_one)
    def first_bases(dtype, coefficients):
        return call(
            functools.partial(base_kernel, scale), shape_of(shared_bases.shape, dtype),
            coefficients, shared_bases, collected_one,
            in_specs=[whole, far, whole], out_specs=far,
            scratch=[columns_spread, wide_scratch, pltpu.VMEM(shared_bases.shape, dtype), sems, sems],
            flops=2 * mix_flops, traffic=2 * base_bytes,
        )

    bases_one = first_bases(bf16, mixing_all)
    panels_one, bases_one = lax.optimization_barrier((panels_one, bases_one))
    sums_one = call(sum_kernel, shape_of((experts, rank), f32), panels_one)
    other_sums = swap_rows(sums_one)
    mine_one = factor_part(low_one, panels_one)
    other_one = swap_rows(mine_one)
    low_two, product_two, gram_two = call(
        step_kernel, products, weights, full, mine_one, other_one,
        flops=wide_flops, traffic=weights.size * 2 + 4 * block_bytes,
    )

    mixed_two, mixing_one, grad_one = call(
        functools.partial(next_mix_kernel, scale), [blocks, small, small], sums_one, other_sums, mixing_all, bases_one,
        in_specs=[whole, whole, whole, far], scratch=[rows_spread, thin_scratch, sems],
        flops=2 * mix_flops, traffic=base_bytes // 2,
    )
    panels_two = exchange(mixed_two)
    collected_two = exchange(panel_part(panels_two.reshape(width, rank), product_two, gram_two))
    mine_two = factor_part(low_two, panels_two)
    other_two = swap_rows(mine_two)
    factors_new = call(
        last_factor_kernel, shape_of((own_rows, rank), f32),
        row, factors, mine_one, other_one, mine_two, other_two,
        in_specs=[scalar] + [whole] * 5, traffic=12 * own_rows * rank,
    )
    partial_two = mixing_part(bases_one, collected_two)
    sums_two = lax.all_to_all(partial_two, ("expert", "row"), split_axis=0, concat_axis=0, tiled=True)
    bases_new = call(
        functools.partial(last_base_kernel, scale), shape_of(shared_bases.shape, f32),
        mixing_all, mixing_one, first_bases(f32, mixing_all), collected_one, collected_two,
        in_specs=[whole, whole, far, whole, whole], out_specs=far,
        scratch=[columns_spread, columns_spread, wide_scratch, sems, sems], flops=4 * mix_flops, traffic=2 * base_bytes,
    )
    mixing_new = call(
        last_mixing_kernel, shape_of(mixing.shape, f32), expert, mixing, grad_one, sums_two,
        in_specs=[scalar] + [whole] * 3,
    )
    return (factors_new[None], bases_new, mixing_new)


def factor_gradient(residual_low, panels):
    grad_factor = jnp.einsum(
        "ehc,ecr->ehr", residual_low, panels, preferred_element_type=jnp.float32
    )
    return lax.psum_scatter(
        grad_factor.astype(jnp.bfloat16), "row", scatter_dimension=1, tiled=True
    ).astype(jnp.float32)


def plain_body(weights, factors, mixing, shared_bases):
    mix_scale = 1.0 / math.sqrt(shared_bases.shape[1] * shared_bases.shape[2])
    local_experts = mixing.shape[0]
    mixing_state = lax.all_gather(mixing, "expert", axis=0, tiled=True)
    factor_state = factors
    factor_one = jnp.zeros(factor_state.shape, jnp.float32)
    factor_two = jnp.zeros(factor_state.shape, jnp.float32)
    mixing_one = jnp.zeros(mixing_state.shape, jnp.float32)
    mixing_two = jnp.zeros(mixing_state.shape, jnp.float32)
    bases_state = shared_bases
    bases_one = jnp.zeros(shared_bases.shape, jnp.float32)
    bases_two = jnp.zeros(shared_bases.shape, jnp.float32)
    for iteration in range(1, ITERS + 1):
        mixing_all = mixing_state
        factor_low = lax.all_gather(factor_state.astype(jnp.bfloat16), "row", axis=1, tiled=True)
        mixed = (
            mix_scale
            * jnp.einsum("ej,cjr->ecr", mixing_all, bases_state, precision=lax.Precision.HIGHEST)
        ).astype(jnp.bfloat16)
        panels = lax.all_to_all(mixed, "expert", split_axis=0, concat_axis=1, tiled=True)
        residual = jnp.einsum(
            "ehr,ecr->ehc", factor_low, panels, preferred_element_type=jnp.float32
        ) - weights.astype(jnp.float32)
        residual_low = residual.astype(jnp.bfloat16)
        grad_panel = jnp.einsum(
            "ehc,ehr->ecr", residual_low, factor_low, preferred_element_type=jnp.float32
        )
        collected = lax.all_to_all(
            grad_panel.astype(jnp.bfloat16), "expert", split_axis=1, concat_axis=0, tiled=True
        ).astype(grad_panel.dtype)
        grad_rows = factor_gradient(residual_low, panels)
        grad_bases = mix_scale * jnp.einsum(
            "ej,ecr->cjr", mixing_all, collected, precision=lax.Precision.HIGHEST
        )
        partial_mixing = mix_scale * jnp.einsum(
            "cjr,ecr->ej", bases_state, collected, precision=lax.Precision.HIGHEST
        )
        bases_state, bases_one, bases_two = adam_update(
            bases_state, bases_one, bases_two, grad_bases, iteration, EPSILON_BASES
        )
        grad_mixing = lax.psum(partial_mixing, ("expert", "row"))
        mixing_state, mixing_one, mixing_two = adam_update(
            mixing_state, mixing_one, mixing_two, grad_mixing, iteration, EPSILON_MIXING
        )
        factor_state, factor_one, factor_two = adam_update(
            factor_state, factor_one, factor_two, grad_rows, iteration, EPSILON_FACTORS
        )
    mixing_out = lax.dynamic_slice_in_dim(
        mixing_state, lax.axis_index("expert") * local_experts, local_experts, 0
    )
    return (factor_state, bases_state, mixing_out)


def body(weights, factors, mixing, shared_bases):
    columns, bases, rank = shared_bases.shape
    experts = weights.shape[2] // columns
    fits = (
        weights.shape[0] == 1
        and weights.shape[1] == 2 * factors.shape[1]
        and columns % CHUNK == 0
        and experts == 8
        and bases == 64
        and rank == 128
        and 2 * experts == TAIL
    )
    run = kernel_body if fits else plain_body
    return run(weights, factors, mixing, shared_bases)


def solution(mesh):
    placed = (
        P(("layer", "expert"), None, "row"),
        P(("layer", "expert"), "row", None),
        P(("layer", "expert"), None),
        P(("layer", "row", "expert"), None, None),
    )
    return jax.shard_map(
        body,
        mesh=mesh,
        in_specs=placed,
        out_specs=(
            P(("layer", "expert"), "row", None),
            P(("layer", "row", "expert"), None, None),
            P(("layer", "expert"), None),
        ),
        check_vma=False,
    )
```

time: 143 us -> 126 us (0.88)
  local copies, waits for them, and re-layouts: 29 us -> 5.39 us
  Pallas kernels: 35.7 us -> 55.8 us
  waiting for transfers between devices: 24.5 us -> 18.2 us
  starting transfers between devices: 20.6 us -> 17.6 us
  blocking collectives: 29.6 us -> 27 us
  other arithmetic: 2.06 us -> 0 us
    unnamed x32 -> x20, local copies, waits for them, and re-layouts: 27.8 us -> 5.39 us
    pallas_call x13 -> x14, Pallas kernels: 35.7 us -> 55.8 us  [call(): pl.pallas_call(kernel, out_shape=out_shape, grid=grid, in_specs=[whole] *...]
    all_to_all x3, waiting for transfers between devices: 19.9 us -> 13.8 us  [exchange(): lax.all_to_all(array, 'expert', split_axis=0, concat_axis=0, tiled=True)]
    all_to_all x1 -> x0, starting transfers between devices: 3.6 us -> none  [kernel_body(): lax.all_to_all(partial_one, ('expert', 'row'), split_axis=0, concat_axis=...]
    all_to_all x2 -> x1, blocking collectives: 29.6 us -> 27 us  [exchange(): lax.all_to_all(array, 'expert', split_axis=0, concat_axis=0, tiled=True)]
    all_to_all x1, starting transfers between devices: 3.74 us -> 5.3 us  [kernel_body(): lax.all_to_all(partial_two, ('expert', 'row'), split_axis=0, concat_axis=...]
    all_to_all x2 -> x0, other arithmetic: 1.5 us -> none  [the longest x1 0.75 us: kernel_body(): lax.all_to_all(partial_two, ('expert', 'row'), split_axis=0, concat_axis=...]
    all_to_all x3, starting transfers between devices: 13 us -> 11.6 us  [exchange(): lax.all_to_all(array, 'expert', split_axis=0, concat_axis=0, tiled=True)]
  transfers between devices with their start and end apart: 8 -> 8, of which waited for: 6 -> 6; matrix products, arithmetic and copies ran while one was open for 0% -> 0% of each run, Pallas kernels for 13% -> 24%
where the time goes in v2:
time: 126 us; the launch traced here: 125 us
  Pallas kernels  55.8 us (44%)
  blocking collectives  27 us (21%)
  waiting for transfers between devices  18.2 us (14%)
  starting transfers between devices  17.6 us (14%)
  local copies, waits for them, and re-layouts  5.39 us (4%)
    pallas_call x14, Pallas kernels, call(): pl.pallas_call(kernel, out_shape=out_shape, grid=grid, in_specs=[whole] *...  55.8 us
    all_to_all x1, blocking collectives, exchange(): lax.all_to_all(array, 'expert', split_axis=0, concat_axis=0, tiled=True)  27 us
    all_to_all x3, waiting for transfers between devices, exchange(): lax.all_to_all(array, 'expert', split_axis=0, concat_axis=0, tiled=True)  13.8 us
    all_to_all x3, starting transfers between devices, exchange(): lax.all_to_all(array, 'expert', split_axis=0, concat_axis=0, tiled=True)  11.6 us
    unnamed x20, local copies, waits for them, and re-layouts  5.39 us
    all_to_all x1, starting transfers between devices, kernel_body(): lax.all_to_all(partial_two, ('expert', 'row'), split_axis=0, concat_axis=...  5.3 us
    ppermute x4, waiting for transfers between devices, swap_rows(): return lax.ppermute(array, 'row', [(0, 1), (1, 0)])  4.42 us
  transfers between devices with their start and end apart: 8, of which 6 were waited for; matrix products, arithmetic and copies ran while one was open for 0% of the time, Pallas kernels for 24%

profile of v2, /device:TPU:0, one launch (start us, length us, event | category | flops | bytes accessed | tf_op | source)
XLA Modules:
  0.0 124.9 jit_solution(12864903708823795220)
XLA Ops:
  0.6 0.5 collective-permute-start
  1.1 1.4 %collective-permute-done.other_ref = f32[512,128]{1,0:T(8,128)S(1)} collective-permute-done((f32[512,128]{1,0:T(8,128)}, f32[512,128]{1,0:T(8,128)S(1)}, u32[]{:S(2)}, u32[]{:S(2)}) %collective-permute-start) | collective-permute-done | bytes 262176 | tf_op jit(solution)/shard_map/ppermute | solution.py:418
  2.5 0.0 copy-start.8
  2.5 0.7 copy-done.8
  3.2 4.7 %shard_map.67 = (f32[1024,128]{1,0:T(8,128)}, bf16[1024,128]{1,0:T(8,128)(2,1)}, bf16[8,368,128]{2,1,0:T(8,128)(2,1)}) custom-call(s32[1]{0:T(128)} %bitcast.row_ref, bf16[1024,1792]{1,0:T(8,128)(2,1)} %bitcast.7, f32[512,128]{1,0:T(8,128)} %bitcast.13, f32[512,128]{1,0:T(8,128)} %copy-done.8, f32[1,64]{1,0:T(1,128)} %mixing_ref.3), custom_call_target="tpu_custom_call" | custom-call | flops 469762048 | bytes 5505024 | tf_op jit(solution)/shard_map/pallas_call | solution.py:124
  7.9 27.0 %all_to_all.25.sent_ref = bf16[8,368,128]{2,1,0:T(8,128)(2,1)} all-to-all(bf16[8,368,128]{2,1,0:T(8,128)(2,1)} %get-tuple-element.18), channel_id=1, replica_groups=mesh['layer'=2,'expert'=8,'row'=2] {'expert'}, dimensions={0} | all-to-all | bytes 1507328 | tf_op jit(solution)/shard_map/all_to_all | solution.py:422
  34.9 10.3 %shard_map.68 = (bf16[8,240,128]{2,1,0:T(8,128)(2,1)}, bf16[8,224,128]{2,1,0:T(8,128)(2,1)}, f32[8,64]{1,0:T(8,128)}) custom-call(bf16[8,368,128]{2,1,0:T(8,128)(2,1)} %all_to_all.25.sent_ref, f32[224,64,128]{2,1,0:T(8,128)} %bases_ref.5), custom_call_target="tpu_custom_call" | custom-call | flops 1409286144 | bytes 7340032 | tf_op jit(solution)/shard_map/pallas_call | solution.py:124
  45.3 3.6 %all-to-all-start.1 = ((bf16[8,240,128]{2,1,0:T(8,128)(2,1)}), bf16[8,240,128]{2,1,0:T(8,128)(2,1)S(1)}, u32[]{:S(2)}, u32[]{:S(2)}) async-start(bf16[8,240,128]{2,1,0:T(8,128)(2,1)} %get-tuple-element.19), calls=%async_computation.1 | async-start | bytes 983040 | tf_op jit(solution)/shard_map/all_to_all | solution.py:422
  48.9 0.0 copy-start.4
  48.9 7.3 %shard_map.69.bases_ref = bf16[224,64,128]{2,1,0:T(8,128)(2,1)} custom-call(f32[8,64]{1,0:T(8,128)} %get-tuple-element.20.mixing_ref.old_ref, f32[224,64,128]{2,1,0:T(8,128)} %bases_ref.5, bf16[8,224,128]{2,1,0:T(8,128)(2,1)} %get-tuple-element.21.blocks_ref.old_blocks_ref), custom_call_target="tpu_custom_call" | custom-call | flops 939524096 | bytes 14680064 | tf_op jit(solution)/shard_map/pallas_call | solution.py:124
  56.3 0.0 copy-start.3
  56.3 6.2 %all-to-all-done.1.panels_ref.sent_ref = bf16[8,240,128]{2,1,0:T(8,128)(2,1)S(1)} async-done(((bf16[8,240,128]{2,1,0:T(8,128)(2,1)}), bf16[8,240,128]{2,1,0:T(8,128)(2,1)S(1)}, u32[]{:S(2)}, u32[]{:S(2)}) %all-to-all-start.1) | async-done | bytes 491552 | tf_op jit(solution)/shard_map/all_to_all | solution.py:422
  62.5 0.0 copy-start.5
  62.5 0.1 collective-permute-start.2
  62.5 1.2 collective-permute-done.2.other_ref
  63.7 0.0 copy-done.5
  63.7 0.0 copy-start.9
  63.7 0.6 copy-done.9
  64.3 4.6 %shard_map.73 = (bf16[8,224,128]{2,1,0:T(8,128)(2,1)}, f32[8,64]{1,0:T(8,128)}, f32[8,64]{1,0:T(8,128)}) custom-call(f32[8,128]{1,0:T(8,128)} %copy-done.5, f32[8,128]{1,0:T(8,128)} %copy-done.9, f32[8,64]{1,0:T(8,128)} %get-tuple-element.20.mixing_ref.old_ref, bf16[224,64,128]{2,1,0:T(8,128)(2,1)} %shard_map.69.bases_ref), custom_call_target="tpu_custom_call" | custom-call | flops 939524096 | bytes 3670016 | tf_op jit(solution)/shard_map/pallas_call | solution.py:124
  68.9 3.6 %all-to-all-start.2 = ((bf16[8,224,128]{2,1,0:T(8,128)(2,1)}), bf16[8,224,128]{2,1,0:T(8,128)(2,1)S(1)}, u32[]{:S(2)}, u32[]{:S(2)}) async-start(bf16[8,224,128]{2,1,0:T(8,128)(2,1)} %get-tuple-element.26), calls=%async_computation.2 | async-start | bytes 917504 | tf_op jit(solution)/shard_map/all_to_all | solution.py:422
  72.6 0.0 copy-done.4
  72.6 0.0 copy-start
  72.6 2.0 %copy-done = bf16[1,1024,1792]{2,1,0:T(8,128)(2,1)S(1)} copy-done((bf16[1,1024,1792]{2,1,0:T(8,128)(2,1)S(1)}, bf16[1,1024,1792]{2,1,0:T(8,128)(2,1)}, u32[]{:S(2)}) %copy-start) | copy-done | bytes 3670040
  74.6 1.5 %shard_map.70.mine_ref.mine_old_ref = f32[1024,128]{1,0:T(8,128)S(1)} custom-call(bf16[1024,1792]{1,0:T(8,128)(2,1)S(1)} %bitcast.8, bf16[1024,128]{1,0:T(8,128)(2,1)S(1)} %copy-done.4, bf16[8,240,128]{2,1,0:T(8,128)(2,1)S(1)} %all-to-all-done.1.panels_ref.sent_ref), custom_call_target="tpu_custom_call" | custom-call | flops 469762048 | bytes 4128768 | tf_op jit(solution)/shard_map/pallas_call | solution.py:124
  76.1 0.1 collective-permute-start.1
  76.2 1.9 %collective-permute-done.1.other_ref.other_old_ref = f32[1024,128]{1,0:T(8,128)S(1)} collective-permute-done((f32[1024,128]{1,0:T(8,128)S(1)}, f32[1024,128]{1,0:T(8,128)S(1)}, u32[]{:S(2)}, u32[]{:S(2)}) %collective-permute-start.1) | collective-permute-done | bytes 524320 | tf_op jit(solution)/shard_map/ppermute | solution.py:418
  78.1 0.0 copy-done.3
  78.1 0.9 shard_map.71
  79.0 7.0 %all-to-all-done.2.panels_ref = bf16[8,224,128]{2,1,0:T(8,128)(2,1)S(1)} async-done(((bf16[8,224,128]{2,1,0:T(8,128)(2,1)}), bf16[8,224,128]{2,1,0:T(8,128)(2,1)S(1)}, u32[]{:S(2)}, u32[]{:S(2)}) %all-to-all-start.2) | async-done | bytes 458784 | tf_op jit(solution)/shard_map/all_to_all | solution.py:422
  86.0 1.2 shard_map.77
  87.2 4.3 %all-to-all-start.3 = ((bf16[8,224,128]{2,1,0:T(8,128)(2,1)}), bf16[8,224,128]{2,1,0:T(8,128)(2,1)}, u32[]{:S(2)}, u32[]{:S(2)}) async-start(bf16[8,224,128]{2,1,0:T(8,128)(2,1)} %bitcast.5), calls=%async_computation.3 | async-start | bytes 917504 | tf_op jit(solution)/shard_map/all_to_all | solution.py:422
  91.5 0.0 copy-start.1
  91.5 2.0 %copy-done.1 = bf16[1,1024,1792]{2,1,0:T(8,128)(2,1)S(1)} copy-done((bf16[1,1024,1792]{2,1,0:T(8,128)(2,1)S(1)}, bf16[1,1024,1792]{2,1,0:T(8,128)(2,1)}, u32[]{:S(2)}) %copy-start.1) | copy-done | bytes 3670040
  93.6 1.5 %shard_map.74.mine_ref = f32[1024,128]{1,0:T(8,128)S(1)} custom-call(bf16[1024,1792]{1,0:T(8,128)(2,1)S(1)} %bitcast.10, bf16[1024,128]{1,0:T(8,128)(2,1)S(1)} %get-tuple-element.24.low_ref, bf16[8,224,128]{2,1,0:T(8,128)(2,1)S(1)} %all-to-all-done.2.panels_ref), custom_call_target="tpu_custom_call" | custom-call | flops 469762048 | bytes 4128768 | tf_op jit(solution)/shard_map/pallas_call | solution.py:124
  95.1 0.1 collective-permute-start.3
  95.2 0.0 copy-start.2
  95.2 7.4 %shard_map.76.bases_ref = f32[224,64,128]{2,1,0:T(8,128)} custom-call(f32[8,64]{1,0:T(8,128)} %get-tuple-element.20.mixing_ref.old_ref, f32[224,64,128]{2,1,0:T(8,128)} %bases_ref.5, bf16[8,224,128]{2,1,0:T(8,128)(2,1)} %get-tuple-element.21.blocks_ref.old_blocks_ref), custom_call_target="tpu_custom_call" | custom-call | flops 939524096 | bytes 14680064 | tf_op jit(solution)/shard_map/pallas_call | solution.py:124
  102.6 0.0 collective-permute-done.3.other_ref
  102.6 0.0 copy-done.2
  102.6 1.0 shard_map.75
  103.6 0.6 all-to-all-done.3.blocks_ref
  104.2 4.7 %shard_map.79 = f32[16,8,128]{2,1,0:T(8,128)} custom-call(bf16[224,64,128]{2,1,0:T(8,128)(2,1)} %shard_map.69.bases_ref, bf16[8,224,128]{2,1,0:T(8,128)(2,1)} %all-to-all-done.3.blocks_ref), custom_call_target="tpu_custom_call" | custom-call | flops 469762048 | bytes 3670016 | tf_op jit(solution)/shard_map/pallas_call | solution.py:124
  109.0 5.3 %all-to-all-start.4 = ((f32[16,8,128]{2,1,0:T(8,128)}), f32[16,8,128]{2,1,0:T(8,128)S(1)}, u32[]{:S(2)}, u32[]{:S(2)}) async-start(f32[16,8,128]{2,1,0:T(8,128)} %shard_map.79), calls=%async_computation.4 | async-start | bytes 131072 | tf_op jit(solution)/shard_map/all_to_all | solution.py:534
  114.3 0.0 copy-start.6
  114.3 0.0 copy-start.7
  114.3 10.0 %shard_map.78 = f32[224,64,128]{2,1,0:T(8,128)} custom-call(f32[8,64]{1,0:T(8,128)} %get-tuple-element.20.mixing_ref.old_ref, f32[8,64]{1,0:T(8,128)} %get-tuple-element.27.new_ref, f32[224,64,128]{2,1,0:T(8,128)} %shard_map.76.bases_ref, bf16[8,224,128]{2,1,0:T(8,128)(2,1)} %get-tuple-element.21.blocks_ref.old_blocks_ref, ...), custom_call_target="tpu_custom_call" | custom-call | flops 1879048192 | bytes 14680064 | tf_op jit(solution)/shard_map/pallas_call | solution.py:124
  124.3 0.0 all-to-all-done.4.sums_ref
  124.3 0.0 copy-done.6
  124.3 0.0 copy-done.7
  124.3 0.6 shard_map.80
  (1 shorter events, 0.0 us)
Async XLA Ops:
  0.6 1.9 %collective-permute-start = (f32[512,128]{1,0:T(8,128)}, f32[512,128]{1,0:T(8,128)S(1)}, u32[]{:S(2)}, u32[]{:S(2)}) collective-permute-start(f32[512,128]{1,0:T(8,128)} %bitcast.12), channel_id=1, source_target_pairs={{0,1},{1,0},{2,3},{3,2},{4,5},{5,4},{6,7},{7,6},{8,9},{9,8},{10,11... | collective-permute-start | bytes 786440 | tf_op jit(solution)/shard_map/ppermute | solution.py:418
  2.5 0.7 copy-start.8
  45.3 17.2 %all-to-all-start.1 = ((bf16[8,240,128]{2,1,0:T(8,128)(2,1)}), bf16[8,240,128]{2,1,0:T(8,128)(2,1)S(1)}, u32[]{:S(2)}, u32[]{:S(2)}) async-start(bf16[8,240,128]{2,1,0:T(8,128)(2,1)} %get-tuple-element.19), calls=%async_computation.1 | async-start | bytes 983040 | tf_op jit(solution)/shard_map/all_to_all | solution.py:422
  48.9 23.6 %copy-start.4 = (bf16[1024,128]{1,0:T(8,128)(2,1)S(1)}, bf16[1024,128]{1,0:T(8,128)(2,1)}, u32[]{:S(2)}) copy-start(bf16[1024,128]{1,0:T(8,128)(2,1)} %get-tuple-element.17.low_ref) | copy-start | bytes 786436
  56.3 21.9 %copy-start.3 = (f32[1024,128]{1,0:T(8,128)S(1)}, f32[1024,128]{1,0:T(8,128)}, u32[]{:S(2)}) copy-start(f32[1024,128]{1,0:T(8,128)} %get-tuple-element.23.full_ref) | copy-start | bytes 1572868
  62.5 1.2 copy-start.5
  62.5 1.2 collective-permute-start.2
  63.7 0.6 copy-start.9
  68.9 17.1 %all-to-all-start.2 = ((bf16[8,224,128]{2,1,0:T(8,128)(2,1)}), bf16[8,224,128]{2,1,0:T(8,128)(2,1)S(1)}, u32[]{:S(2)}, u32[]{:S(2)}) async-start(bf16[8,224,128]{2,1,0:T(8,128)(2,1)} %get-tuple-element.26), calls=%async_computation.2 | async-start | bytes 917504 | tf_op jit(solution)/shard_map/all_to_all | solution.py:422
  72.6 2.0 %copy-start = (bf16[1,1024,1792]{2,1,0:T(8,128)(2,1)S(1)}, bf16[1,1024,1792]{2,1,0:T(8,128)(2,1)}, u32[]{:S(2)}) copy-start(bf16[1,1024,1792]{2,1,0:T(8,128)(2,1)} %param.4) | copy-start | bytes 11010052
  76.1 2.0 %collective-permute-start.1 = (f32[1024,128]{1,0:T(8,128)S(1)}, f32[1024,128]{1,0:T(8,128)S(1)}, u32[]{:S(2)}, u32[]{:S(2)}) collective-permute-start(f32[1024,128]{1,0:T(8,128)S(1)} %shard_map.70.mine_ref.mine_old_ref), channel_id=1, source_target_pairs={{0,1},{1,0},{2,3},{3,2},{4,5},{5,4},{6,7},{7,6},{8,9},{9,8},{10,11... | collective-permute-start | bytes 1572872 | tf_op jit(solution)/shard_map/ppermute | solution.py:418
  87.2 17.0 %all-to-all-start.3 = ((bf16[8,224,128]{2,1,0:T(8,128)(2,1)}), bf16[8,224,128]{2,1,0:T(8,128)(2,1)}, u32[]{:S(2)}, u32[]{:S(2)}) async-start(bf16[8,224,128]{2,1,0:T(8,128)(2,1)} %bitcast.5), calls=%async_computation.3 | async-start | bytes 917504 | tf_op jit(solution)/shard_map/all_to_all | solution.py:422
  91.5 2.0 %copy-start.1 = (bf16[1,1024,1792]{2,1,0:T(8,128)(2,1)S(1)}, bf16[1,1024,1792]{2,1,0:T(8,128)(2,1)}, u32[]{:S(2)}) copy-start(bf16[1,1024,1792]{2,1,0:T(8,128)(2,1)} %param.4) | copy-start | bytes 11010052
  95.1 7.5 %collective-permute-start.3 = (f32[1024,128]{1,0:T(8,128)S(1)}, f32[1024,128]{1,0:T(8,128)S(1)}, u32[]{:S(2)}, u32[]{:S(2)}) collective-permute-start(f32[1024,128]{1,0:T(8,128)S(1)} %shard_map.74.mine_ref), channel_id=1, source_target_pairs={{0,1},{1,0},{2,3},{3,2},{4,5},{5,4},{6,7},{7,6},{8,9},{9,8},{10,11... | collective-permute-start | bytes 1572872 | tf_op jit(solution)/shard_map/ppermute | solution.py:418
  95.2 7.5 %copy-start.2 = (f32[1,512,128]{2,1,0:T(8,128)S(1)}, f32[1,512,128]{2,1,0:T(8,128)}, u32[]{:S(2)}) copy-start(f32[1,512,128]{2,1,0:T(8,128)} %param.5) | copy-start | bytes 786436
  109.0 15.3 %all-to-all-start.4 = ((f32[16,8,128]{2,1,0:T(8,128)}), f32[16,8,128]{2,1,0:T(8,128)S(1)}, u32[]{:S(2)}, u32[]{:S(2)}) async-start(f32[16,8,128]{2,1,0:T(8,128)} %shard_map.79), calls=%async_computation.4 | async-start | bytes 131072 | tf_op jit(solution)/shard_map/all_to_all | solution.py:534
  114.3 10.0 %copy-start.6 = (f32[8,64]{1,0:T(8,128)S(1)}, f32[8,64]{1,0:T(8,128)}, u32[]{:S(2)}) copy-start(f32[8,64]{1,0:T(8,128)} %get-tuple-element.30.old_ref) | copy-start | bytes 6148
  114.3 10.0 %copy-start.7 = (f32[1,64]{1,0:T(1,128)S(1)}, f32[1,64]{1,0:T(1,128)}, u32[]{:S(2)}) copy-start(f32[1,64]{1,0:T(1,128)} %mixing_ref.3) | copy-start | bytes 772

commit v3 on v2

--- a/solution.py
+++ b/solution.py
@@ -118,7 +118,7 @@
     return specs is not None and any(spec.memory_space == pltpu.HBM for spec in specs)
 
 
-def call(kernel, out_shape, *args, grid=(), in_specs=None, out_specs=None, scratch=(), flops=0, traffic=0, limit=24):
+def call(kernel, out_shape, *args, grid=(), in_specs=None, out_specs=None, scratch=(), flops=0, traffic=0, limit=20):
     whole = pl.BlockSpec(memory_space=pltpu.VMEM)
     single = isinstance(out_shape, jax.ShapeDtypeStruct)
     return pl.pallas_call(
@@ -143,23 +143,21 @@
 
 
 def start_kernel(
-    row_ref, far_weights_ref, own_ref, other_ref, mixing_ref, full_ref, low_ref, out_ref, weights_ref, sem
+    weights_ref, full_ref, mixing_ref, low_ref, out_ref
 ):
-    load = pltpu.make_async_copy(far_weights_ref, weights_ref, sem)
-    load.start()
-    rows = own_ref.shape[0]
-    row = row_ref[0]
-    full_ref[pl.ds(pl.multiple_of(row * rows, rows), rows), :] = own_ref[...]
-    full_ref[pl.ds(pl.multiple_of((1 - row) * rows, rows), rows), :] = other_ref[...]
     low = full_ref[...].astype(jnp.bfloat16)
     low_ref[...] = low
     experts, height, rank = out_ref.shape
-    columns = height - rank - TAIL
+    half = rank // 2
+    end = height - TAIL
+    columns = end - rank - half
     gram = dot(low, low, ((0,), (0,)))
-    high = gram.astype(jnp.bfloat16)
-    out_ref[:, columns : columns + rank, :] = jnp.broadcast_to(high[None], (experts, rank, rank))
-    diagonal = lax.broadcasted_iota(jnp.int32, gram.shape, 0) == lax.broadcasted_iota(jnp.int32, gram.shape, 1)
-    rest = jnp.sum(jnp.where(diagonal, gram - high.astype(jnp.float32), 0.0), axis=0, keepdims=True)
+    packed = []
+    for part in halves(gram):
+        corner = jnp.concatenate([part[half : half + half // 2, half:], part[half + half // 2 :, half:]], axis=1)
+        packed += [part[:half], corner]
+    packed = jnp.concatenate(packed, axis=0)
+    out_ref[:, columns:end, :] = jnp.broadcast_to(packed[None], (experts,) + packed.shape)
     mixing = mixing_ref[...]
     mixing = jnp.concatenate([mixing, jnp.zeros((1, rank - mixing.shape[1]), jnp.float32)], axis=1)
     first = mixing.astype(jnp.bfloat16).astype(jnp.float32)
@@ -167,10 +165,9 @@
     third = mixing - first - second
     place = lax.broadcasted_iota(jnp.int32, (TAIL, rank), 0)
     tail = jnp.zeros((TAIL, rank), jnp.float32)
-    for position, part in enumerate((first, second, third, rest)):
+    for position, part in enumerate((first, second, third)):
         tail = jnp.where(place == position, part, tail)
-    out_ref[:, columns + rank :, :] = jnp.broadcast_to(tail.astype(jnp.bfloat16)[None], (experts, TAIL, rank))
-    load.wait()
+    out_ref[:, end:, :] = jnp.broadcast_to(tail.astype(jnp.bfloat16)[None], (experts, TAIL, rank))
     product = dot(low, weights_ref[...], ((0,), (0,))).T.astype(jnp.bfloat16)
     out_ref[:, :columns, :] = product.reshape(experts, columns, rank)
 
@@ -242,16 +239,6 @@
     each_pair(source.shape[0], lambda pair: copy_of(source, target, sems, pair).wait())
 
 
-def run_pairs(source, target, sems, step, batch=3):
-    count = source.shape[0] // CHUNK
-    for first in range(0, count, batch):
-        batch_pairs = range(first, min(first + batch, count))
-        for pair in batch_pairs:
-            copy_of(source, target, sems, pair).wait()
-        for pair in batch_pairs:
-            step(pair)
-
-
 def low_pair(ref, pair):
     return jnp.concatenate([part.astype(jnp.bfloat16) for part in pair_of(ref, pair)], axis=1)
 
@@ -261,26 +248,13 @@
     return [jnp.concatenate(side, axis=1) for side in zip(*parts)]
 
 
-def mix_groups(spread, bases_ref, bases, sems, out_ref):
-    half = spread.shape[0] // 2
-    rank = bases.shape[-1]
-
-    def step(pair):
-        if bases.dtype == jnp.float32:
-            high, low = low_rest_pair(bases, pair)
-            both = dot(spread[...], high)
-            mixed = both[:half] + both[half:] + dot(spread[:half], low)
-        else:
-            both = dot(spread[...], low_pair(bases, pair))
-            mixed = both[:half] + both[half:]
-        mixed = mixed.astype(jnp.bfloat16)
-        start = pair * CHUNK
-        for part in range(2):
-            out_ref[:, pl.ds(start + part * GROUP, GROUP), :] = mixed[:, part * rank : (part + 1) * rank].reshape(
-                -1, GROUP, rank
-            )
-
-    run_pairs(bases_ref, bases, sems, step)
+def put_mixed(out_ref, pair, wide):
+    wide = wide.astype(jnp.bfloat16)
+    rank = wide.shape[1] // 2
+    start = pl.multiple_of(pair * CHUNK, CHUNK)
+    for part in range(2):
+        mixed = wide[:, part * rank : (part + 1) * rank]
+        out_ref[:, pl.ds(start + part * GROUP, GROUP), :] = mixed.reshape(-1, GROUP, rank)
 
 
 def fold_total(scale, total, lanes):
@@ -300,33 +274,54 @@
     )
 
 
-def first_kernel(scale, sent_ref, bases_ref, out_ref, blocks_ref, mixing_ref, spread, total, blocks_rest, bases, sems):
+def first_kernel(
+    scale, sent_ref, bases_ref, out_ref, blocks_ref, mixing_ref,
+    spread, total, wide_blocks, grams, high_bases, low_bases, bases, sems,
+):
     start_copies(bases_ref, bases, sems)
     columns, count, rank = bases.shape
     experts = sent_ref.shape[0]
-    tail = sent_ref[:, columns + rank :, :].astype(jnp.float32)
+    half = rank // 2
+    for index in range(2 * experts):
+        expert, start = index // 2, columns + (index % 2) * (half + half // 2)
+        top = sent_ref[expert, start : start + half, :]
+        packed = sent_ref[expert, start + half : start + half + half // 2, :]
+        grams[index, :half, :] = top
+        corner = jnp.concatenate([packed[:, :half], packed[:, half:]], axis=0)
+        side = top[:, half:].astype(jnp.float32).T.astype(jnp.bfloat16)
+        grams[index, half:, :] = jnp.concatenate([side, corner], axis=1)
+    tail = sent_ref[:, columns + rank + half :, :].astype(jnp.float32)
     place = lax.broadcasted_iota(jnp.int32, tail.shape, 1)
     mixing = jnp.sum(jnp.where(place < 3, tail, 0.0), axis=1)[:, :count]
-    rest = jnp.sum(jnp.where(place == 3, tail, 0.0), axis=1)
     mixing_ref[...] = mixing
     spread[...] = spread_rows(mixing, scale)
-    mix_groups(spread, bases_ref, bases, sems, out_ref)
+    half = spread.shape[0] // 2
+
+    def mix(pair):
+        copy_of(bases_ref, bases, sems, pair).wait()
+        high, low = low_rest_pair(bases, pair)
+        here = pl.ds(pl.multiple_of(pair * 2 * rank, 2 * rank), 2 * rank)
+        high_bases[:, here] = high
+        low_bases[:, here] = low
+        both = dot(spread[...], high)
+        put_mixed(out_ref, pair, both[:half] + both[half:] + dot(spread[:half], low))
+
+    each_pair(columns, mix)
     for expert in range(experts):
         mixed = out_ref[expert, :columns, :]
-        blocks_ref[expert], blocks_rest[expert] = halves(
-            dot(mixed, sent_ref[expert, columns : columns + rank, :])
-            + mixed.astype(jnp.float32) * rest[expert : expert + 1]
+        high, low = halves(
+            dot(mixed, grams[2 * expert])
+            + dot(mixed, grams[2 * expert + 1])
             - sent_ref[expert, :columns, :].astype(jnp.float32)
         )
-    half = total.shape[0]
-    result = None
-    for pair in range(columns // CHUNK):
-        high, low = low_rest_pair(bases, pair)
-        blocks = blocks_of(blocks_ref, pair)
-        both = dot(jnp.concatenate([blocks, blocks_of(blocks_rest, pair)], axis=0), high, ((1,), (1,)))
-        product = both[:half] + both[half:] + dot(blocks, low, ((1,), (1,)))
-        result = product if result is None else result + product
-    total[...] = result
+        blocks_ref[expert] = high
+        for position in range(columns // GROUP):
+            rows = slice(position * GROUP, (position + 1) * GROUP)
+            lanes = slice(position * rank, (position + 1) * rank)
+            wide_blocks[expert * GROUP : (expert + 1) * GROUP, lanes] = high[rows]
+            wide_blocks[half + expert * GROUP : half + (expert + 1) * GROUP, lanes] = low[rows]
+    both = dot(wide_blocks[...], high_bases[...], ((1,), (1,)))
+    total[...] = both[:half] + both[half:] + dot(wide_blocks[:half], low_bases[...], ((1,), (1,)))
     high, low = halves(fold_total(scale, total, rank))
     sums = jnp.concatenate([high, low], axis=0)
     out_ref[:, columns:, :] = jnp.broadcast_to(sums[None], (experts,) + sums.shape)
@@ -339,25 +334,24 @@
     out_ref[...] = sums[:experts] + sums[experts:]
 
 
-def next_mix_kernel(scale, mine_ref, other_ref, mixing_ref, bases_ref, out_ref, next_ref, grad_ref, spread, bases, sems):
-    start_copies(bases_ref, bases, sems)
+def next_mix_kernel(scale, mine_ref, other_ref, mixing_ref, bases_ref, out_ref, next_ref, grad_ref, spread):
     mixing = mixing_ref[...]
     gradient = (mine_ref[...] + other_ref[...])[:, : mixing.shape[1]]
     following = first_step(mixing, gradient, EPSILON_MIXING)
     next_ref[...] = following
     grad_ref[...] = gradient
     spread[...] = spread_rows(following, scale)
-    mix_groups(spread, bases_ref, bases, sems, out_ref)
-
-
-def mixing_kernel(scale, bases_ref, blocks_ref, out_ref, total, bases, sems):
-    start_copies(bases_ref, bases, sems)
-    total[...] = jnp.zeros_like(total)
-
-    def step(pair):
-        total[...] += dot(blocks_of(blocks_ref, pair), low_pair(bases, pair), ((1,), (1,)))
-
-    run_pairs(bases_ref, bases, sems, step)
+    half = spread.shape[0] // 2
+    for pair in range(bases_ref.shape[0] // CHUNK):
+        both = dot(spread[...], low_pair(bases_ref, pair))
+        put_mixed(out_ref, pair, both[:half] + both[half:])
+
+
+def mixing_kernel(scale, bases_ref, blocks_ref, out_ref, total):
+    total[...] = sum(
+        dot(blocks_of(blocks_ref, pair), low_pair(bases_ref, pair), ((1,), (1,)))
+        for pair in range(bases_ref.shape[0] // CHUNK)
+    )
     gradient = fold_total(scale, total, out_ref.shape[-1])
     out_ref[...] = jnp.broadcast_to(gradient[None], out_ref.shape)
 
@@ -445,7 +439,6 @@
     far = pl.BlockSpec(memory_space=pltpu.HBM)
     sems = pltpu.SemaphoreType.DMA((columns // CHUNK,))
     wide_scratch = pltpu.VMEM(shared_bases.shape, f32)
-    thin_scratch = pltpu.VMEM(shared_bases.shape, bf16)
     blocks = shape_of((experts, columns, rank), bf16)
     panels_shape = shape_of((width, rank), bf16)
     small = shape_of((experts, bases), f32)
@@ -468,19 +461,15 @@
         return call(
             functools.partial(mixing_kernel, scale),
             shape_of((devices, experts, rank), f32), values, collected,
-            in_specs=[far, whole],
-            scratch=[
-                pltpu.VMEM((experts * GROUP, GROUP * bases), f32), pltpu.VMEM(values.shape, values.dtype), sems
-            ],
+            scratch=[pltpu.VMEM((experts * GROUP, GROUP * bases), f32)],
             flops=mix_flops, traffic=values.size * values.dtype.itemsize,
         )
 
-    full, low_one, sent = call(
+    full = lax.all_gather(factors, "row", axis=0, tiled=True)
+    low_one, sent = call(
         start_kernel,
-        [shape_of((height, rank), f32), products[0], shape_of((experts, columns + rank + TAIL, rank), bf16)],
-        row, weights, factors, swap_rows(factors), mixing,
-        in_specs=[scalar, far] + [whole] * 3,
-        scratch=[pltpu.VMEM(weights.shape, bf16), pltpu.SemaphoreType.DMA(())],
+        [products[0], shape_of((experts, columns + 3 * rank // 2 + TAIL, rank), bf16)],
+        weights, full, mixing,
         flops=wide_flops, traffic=weights.size * 2 + 4 * block_bytes,
     )
 
@@ -490,7 +479,9 @@
         [shape_of((experts, columns + 2 * experts, rank), bf16), blocks, small], sent, shared_bases,
         in_specs=[whole, far],
         scratch=[
-            rows_spread, pltpu.VMEM((experts * GROUP, GROUP * bases), f32), pltpu.VMEM(blocks.shape, bf16),
+            rows_spread, pltpu.VMEM((experts * GROUP, GROUP * bases), f32),
+            pltpu.VMEM((2 * experts * GROUP, columns // GROUP * rank), bf16),
+            pltpu.VMEM((2 * experts, rank, rank), bf16), *[pltpu.VMEM((GROUP * bases, columns // GROUP * rank), bf16)] * 2,
             wide_scratch, sems,
         ],
         flops=3 * mix_flops, traffic=base_bytes,
@@ -518,7 +509,7 @@
 
     mixed_two, mixing_one, grad_one = call(
         functools.partial(next_mix_kernel, scale), [blocks, small, small], sums_one, other_sums, mixing_all, bases_one,
-        in_specs=[whole, whole, whole, far], scratch=[rows_spread, thin_scratch, sems],
+        scratch=[rows_spread],
         flops=2 * mix_flops, traffic=base_bytes // 2,
     )
     panels_two = exchange(mixed_two)

time: 126 us -> 125 us (level)
  Pallas kernels: 55.8 us -> 45.8 us
  local copies, waits for them, and re-layouts: 5.39 us -> 11.5 us
  blocking collectives: 27 us -> 32.6 us
  starting transfers between devices: 17.6 us -> 16 us
    pallas_call x14, Pallas kernels: 55.8 us -> 45.8 us  [call(): pl.pallas_call(kernel, out_shape=out_shape, grid=grid, in_specs=[whole] *...]
    unnamed x20 -> x22, local copies, waits for them, and re-layouts: 5.39 us -> 11.5 us
    all_to_all x1, blocking collectives: 27 us -> 30.1 us  [exchange(): lax.all_to_all(array, 'expert', split_axis=0, concat_axis=0, tiled=True)]
    all_gather x0 -> x1, blocking collectives: none -> 2.47 us  [kernel_body(): full = lax.all_gather(factors, 'row', axis=0, tiled=True)]
    ppermute x4 -> x3, waiting for transfers between devices: 4.42 us -> 3.05 us  [swap_rows(): return lax.ppermute(array, 'row', [(0, 1), (1, 0)])]
  transfers between devices with their start and end apart: 8 -> 7, of which waited for: 6 -> 5; matrix products, arithmetic and copies ran while one was open for 0% -> 0% of each run, Pallas kernels for 24% -> 24%
where the time goes in v3:
time: 125 us; the launch traced here: 124 us
  Pallas kernels  45.8 us (37%)
  blocking collectives  32.6 us (26%)
  waiting for transfers between devices  17.3 us (14%)
  starting transfers between devices  16 us (13%)
  local copies, waits for them, and re-layouts  11.5 us (9%)
    pallas_call x14, Pallas kernels, call(): pl.pallas_call(kernel, out_shape=out_shape, grid=grid, in_specs=[whole] *...  45.8 us
    all_to_all x1, blocking collectives, exchange(): lax.all_to_all(array, 'expert', split_axis=0, concat_axis=0, tiled=True)  30.1 us
    all_to_all x3, waiting for transfers between devices, exchange(): lax.all_to_all(array, 'expert', split_axis=0, concat_axis=0, tiled=True)  14.2 us
    unnamed x22, local copies, waits for them, and re-layouts  11.5 us
    all_to_all x3, starting transfers between devices, exchange(): lax.all_to_all(array, 'expert', split_axis=0, concat_axis=0, tiled=True)  10.8 us
    all_to_all x1, starting transfers between devices, kernel_body(): lax.all_to_all(partial_two, ('expert', 'row'), split_axis=0, concat_axis=...  5.01 us
    ppermute x3, waiting for transfers between devices, swap_rows(): return lax.ppermute(array, 'row', [(0, 1), (1, 0)])  3.05 us
  transfers between devices with their start and end apart: 7, of which 5 were waited for; matrix products, arithmetic and copies ran while one was open for 0% of the time, Pallas kernels for 24%

profile of v3, /device:TPU:0, one launch (start us, length us, event | category | flops | bytes accessed | tf_op | source)
XLA Modules:
  0.0 123.9 jit_solution(9367876554885653292)
XLA Ops:
  0.6 2.5 %all-gather = f32[1,1024,128]{2,1,0:T(8,128)S(1)} all-gather(f32[1,512,128]{2,1,0:T(8,128)} %param.5), channel_id=2, replica_groups=mesh['layer'=2,'expert'=8,'row'=2] {'row'}, dimensions={1}, use_global_device_ids=true | all-gather | bytes 786432 | tf_op jit(solution)/shard_map/all_gather | solution.py:468
  3.1 0.0 copy-start
  3.1 2.0 %copy-done = bf16[1,1024,1792]{2,1,0:T(8,128)(2,1)S(1)} copy-done((bf16[1,1024,1792]{2,1,0:T(8,128)(2,1)S(1)}, bf16[1,1024,1792]{2,1,0:T(8,128)(2,1)}, u32[]{:S(2)}) %copy-start) | copy-done | bytes 3670040
  5.1 0.0 copy-start.9
  5.1 0.7 copy-done.9
  5.8 0.8 shard_map.67
  6.6 30.1 %all_to_all.25.sent_ref = bf16[8,432,128]{2,1,0:T(8,128)(2,1)} all-to-all(bf16[8,432,128]{2,1,0:T(8,128)(2,1)S(1)} %get-tuple-element.17), channel_id=1, replica_groups=mesh['layer'=2,'expert'=8,'row'=2] {'expert'}, dimensions={0} | all-to-all | bytes 1769472 | tf_op jit(solution)/shard_map/all_to_all | solution.py:416
  36.7 9.0 %shard_map.68 = (bf16[8,240,128]{2,1,0:T(8,128)(2,1)}, bf16[8,224,128]{2,1,0:T(8,128)(2,1)}, f32[8,64]{1,0:T(8,128)}) custom-call(bf16[8,432,128]{2,1,0:T(8,128)(2,1)} %all_to_all.25.sent_ref, f32[224,64,128]{2,1,0:T(8,128)} %bases_ref.5), custom_call_target="tpu_custom_call" | custom-call | flops 1409286144 | bytes 7340032 | tf_op jit(solution)/shard_map/pallas_call | solution.py:124
  45.7 0.0 copy-start.7
  45.7 3.5 %all-to-all-start.1 = ((bf16[8,240,128]{2,1,0:T(8,128)(2,1)}), bf16[8,240,128]{2,1,0:T(8,128)(2,1)S(1)}, u32[]{:S(2)}, u32[]{:S(2)}) async-start(bf16[8,240,128]{2,1,0:T(8,128)(2,1)} %get-tuple-element.18), calls=%async_computation.1 | async-start | bytes 983040 | tf_op jit(solution)/shard_map/all_to_all | solution.py:416
  49.2 7.3 %shard_map.69.bases_ref = bf16[224,64,128]{2,1,0:T(8,128)(2,1)} custom-call(f32[8,64]{1,0:T(8,128)} %get-tuple-element.19.mixing_ref.old_ref, f32[224,64,128]{2,1,0:T(8,128)} %bases_ref.5, bf16[8,224,128]{2,1,0:T(8,128)(2,1)} %get-tuple-element.20.blocks_ref.old_blocks_ref), custom_call_target="tpu_custom_call" | custom-call | flops 939524096 | bytes 14680064 | tf_op jit(solution)/shard_map/pallas_call | solution.py:124
  56.5 6.1 %all-to-all-done.1.panels_ref.sent_ref = bf16[8,240,128]{2,1,0:T(8,128)(2,1)S(1)} async-done(((bf16[8,240,128]{2,1,0:T(8,128)(2,1)}), bf16[8,240,128]{2,1,0:T(8,128)(2,1)S(1)}, u32[]{:S(2)}, u32[]{:S(2)}) %all-to-all-start.1) | async-done | bytes 491552 | tf_op jit(solution)/shard_map/all_to_all | solution.py:416
  62.6 0.1 collective-permute-start.1
  62.7 1.2 collective-permute-done.1.other_ref
  63.8 0.0 copy-done.7
  63.8 0.0 copy-start.3
  63.8 2.0 %copy-done.3 = bf16[224,64,128]{2,1,0:T(8,128)(2,1)S(1)} copy-done((bf16[224,64,128]{2,1,0:T(8,128)(2,1)S(1)}, bf16[224,64,128]{2,1,0:T(8,128)(2,1)}, u32[]{:S(2)}) %copy-start.3) | copy-done | bytes 3670040
  65.9 2.4 %shard_map.73 = (bf16[8,224,128]{2,1,0:T(8,128)(2,1)}, f32[8,64]{1,0:T(8,128)S(1)}, f32[8,64]{1,0:T(8,128)S(1)}) custom-call(f32[8,128]{1,0:T(8,128)S(1)} %shard_map.72.mine_ref, f32[8,128]{1,0:T(8,128)S(1)} %collective-permute-done.1.other_ref, f32[8,64]{1,0:T(8,128)S(1)} %copy-done.7, bf16[224,64,128]{2,1,0:T(8,128)(2,1)S(1)} %copy-done.3), custom_call_target="tpu_custom_call" | custom-call | flops 939524096 | bytes 3670016 | tf_op jit(solution)/shard_map/pallas_call | solution.py:124
  68.2 0.0 copy-start.8
  68.2 0.6 copy-done.8
  68.8 3.6 %all-to-all-start.2 = ((bf16[8,224,128]{2,1,0:T(8,128)(2,1)}), bf16[8,224,128]{2,1,0:T(8,128)(2,1)S(1)}, u32[]{:S(2)}, u32[]{:S(2)}) async-start(bf16[8,224,128]{2,1,0:T(8,128)(2,1)} %get-tuple-element.24), calls=%async_computation.2 | async-start | bytes 917504 | tf_op jit(solution)/shard_map/all_to_all | solution.py:416
  72.5 0.0 copy-start.1
  72.5 2.0 %copy-done.1 = bf16[1,1024,1792]{2,1,0:T(8,128)(2,1)S(1)} copy-done((bf16[1,1024,1792]{2,1,0:T(8,128)(2,1)S(1)}, bf16[1,1024,1792]{2,1,0:T(8,128)(2,1)}, u32[]{:S(2)}) %copy-start.1) | copy-done | bytes 3670040
  74.5 1.5 %shard_map.70.mine_ref.mine_old_ref = f32[1024,128]{1,0:T(8,128)S(1)} custom-call(bf16[1024,1792]{1,0:T(8,128)(2,1)S(1)} %bitcast.9, bf16[1024,128]{1,0:T(8,128)(2,1)S(1)} %get-tuple-element.16.low_ref, bf16[8,240,128]{2,1,0:T(8,128)(2,1)S(1)} %all-to-all-done.1.panels_ref.sent_ref), custom_call_target="tpu_custom_call" | custom-call | flops 469762048 | bytes 4128768 | tf_op jit(solution)/shard_map/pallas_call | solution.py:124
  76.0 0.1 collective-permute-start
  76.1 1.9 %collective-permute-done.other_ref.other_old_ref = f32[1024,128]{1,0:T(8,128)S(1)} collective-permute-done((f32[1024,128]{1,0:T(8,128)S(1)}, f32[1024,128]{1,0:T(8,128)S(1)}, u32[]{:S(2)}, u32[]{:S(2)}) %collective-permute-start) | collective-permute-done | bytes 524320 | tf_op jit(solution)/shard_map/ppermute | solution.py:412
  78.0 0.9 shard_map.71
  78.9 7.0 %all-to-all-done.2.panels_ref = bf16[8,224,128]{2,1,0:T(8,128)(2,1)S(1)} async-done(((bf16[8,224,128]{2,1,0:T(8,128)(2,1)}), bf16[8,224,128]{2,1,0:T(8,128)(2,1)S(1)}, u32[]{:S(2)}, u32[]{:S(2)}) %all-to-all-start.2) | async-done | bytes 458784 | tf_op jit(solution)/shard_map/all_to_all | solution.py:416
  85.9 1.2 shard_map.77
  87.1 3.7 %all-to-all-start.3 = ((bf16[8,224,128]{2,1,0:T(8,128)(2,1)}), bf16[8,224,128]{2,1,0:T(8,128)(2,1)S(1)}, u32[]{:S(2)}, u32[]{:S(2)}) async-start(bf16[8,224,128]{2,1,0:T(8,128)(2,1)} %bitcast.6), calls=%async_computation.3 | async-start | bytes 917504 | tf_op jit(solution)/shard_map/all_to_all | solution.py:416
  90.8 0.0 copy-start.2
  90.8 2.0 %copy-done.2 = bf16[1,1024,1792]{2,1,0:T(8,128)(2,1)S(1)} copy-done((bf16[1,1024,1792]{2,1,0:T(8,128)(2,1)S(1)}, bf16[1,1024,1792]{2,1,0:T(8,128)(2,1)}, u32[]{:S(2)}) %copy-start.2) | copy-done | bytes 3670040
  92.8 1.5 %shard_map.74.mine_ref = f32[1024,128]{1,0:T(8,128)S(1)} custom-call(bf16[1024,1792]{1,0:T(8,128)(2,1)S(1)} %bitcast.11, bf16[1024,128]{1,0:T(8,128)(2,1)S(1)} %get-tuple-element.22.low_ref, bf16[8,224,128]{2,1,0:T(8,128)(2,1)S(1)} %all-to-all-done.2.panels_ref), custom_call_target="tpu_custom_call" | custom-call | flops 469762048 | bytes 4128768 | tf_op jit(solution)/shard_map/pallas_call | solution.py:124
  94.4 0.1 collective-permute-start.2
  94.4 0.0 copy-start.6
  94.5 7.4 %shard_map.76.bases_ref = f32[224,64,128]{2,1,0:T(8,128)} custom-call(f32[8,64]{1,0:T(8,128)} %get-tuple-element.19.mixing_ref.old_ref, f32[224,64,128]{2,1,0:T(8,128)} %bases_ref.5, bf16[8,224,128]{2,1,0:T(8,128)(2,1)} %get-tuple-element.20.blocks_ref.old_blocks_ref), custom_call_target="tpu_custom_call" | custom-call | flops 939524096 | bytes 14680064 | tf_op jit(solution)/shard_map/pallas_call | solution.py:124
  101.9 0.0 collective-permute-done.2.other_ref
  101.9 0.0 copy-done.6
  101.9 1.0 shard_map.75
  102.9 1.1 all-to-all-done.3.blocks_ref
  104.0 0.0 copy-start.4
  104.0 2.0 %copy-done.4 = bf16[224,64,128]{2,1,0:T(8,128)(2,1)S(1)} copy-done((bf16[224,64,128]{2,1,0:T(8,128)(2,1)S(1)}, bf16[224,64,128]{2,1,0:T(8,128)(2,1)}, u32[]{:S(2)}) %copy-start.4) | copy-done | bytes 3670040
  106.1 0.0 copy-start.5
  106.1 2.3 %shard_map.79 = f32[16,8,128]{2,1,0:T(8,128)} custom-call(bf16[224,64,128]{2,1,0:T(8,128)(2,1)S(1)} %copy-done.4, bf16[8,224,128]{2,1,0:T(8,128)(2,1)S(1)} %all-to-all-done.3.blocks_ref), custom_call_target="tpu_custom_call" | custom-call | flops 469762048 | bytes 3670016 | tf_op jit(solution)/shard_map/pallas_call | solution.py:124
  108.3 5.0 %all-to-all-start.4 = ((f32[16,8,128]{2,1,0:T(8,128)}), f32[16,8,128]{2,1,0:T(8,128)S(1)}, u32[]{:S(2)}, u32[]{:S(2)}) async-start(f32[16,8,128]{2,1,0:T(8,128)} %shard_map.79), calls=%async_computation.4 | async-start | bytes 131072 | tf_op jit(solution)/shard_map/all_to_all | solution.py:525
  113.3 0.0 copy-done.5
  113.3 0.0 copy-start.10
  113.3 10.0 %shard_map.78 = f32[224,64,128]{2,1,0:T(8,128)} custom-call(f32[8,64]{1,0:T(8,128)} %get-tuple-element.19.mixing_ref.old_ref, f32[8,64]{1,0:T(8,128)} %copy-done.8, f32[224,64,128]{2,1,0:T(8,128)} %shard_map.76.bases_ref, bf16[8,224,128]{2,1,0:T(8,128)(2,1)} %get-tuple-element.20.blocks_ref.old_blocks_ref, bf16[8,224,128]{2,1,0:T(8,128)(2,1)} %copy-done.5), custom_call_target="tpu_custom_call" | custom-call | flops 1879048192 | bytes 14680064 | tf_op jit(solution)/shard_map/pallas_call | solution.py:124
  123.3 0.0 all-to-all-done.4.sums_ref
  123.3 0.0 copy-done.10
  123.4 0.6 shard_map.80
  (1 shorter events, 0.0 us)
Async XLA Ops:
  3.1 2.0 %copy-start = (bf16[1,1024,1792]{2,1,0:T(8,128)(2,1)S(1)}, bf16[1,1024,1792]{2,1,0:T(8,128)(2,1)}, u32[]{:S(2)}) copy-start(bf16[1,1024,1792]{2,1,0:T(8,128)(2,1)} %param.4) | copy-start | bytes 11010052
  5.1 0.7 copy-start.9
  45.7 18.1 %copy-start.7 = (f32[8,64]{1,0:T(8,128)S(1)}, f32[8,64]{1,0:T(8,128)}, u32[]{:S(2)}) copy-start(f32[8,64]{1,0:T(8,128)} %get-tuple-element.19.mixing_ref.old_ref) | copy-start | bytes 6148
  45.7 16.9 %all-to-all-start.1 = ((bf16[8,240,128]{2,1,0:T(8,128)(2,1)}), bf16[8,240,128]{2,1,0:T(8,128)(2,1)S(1)}, u32[]{:S(2)}, u32[]{:S(2)}) async-start(bf16[8,240,128]{2,1,0:T(8,128)(2,1)} %get-tuple-element.18), calls=%async_computation.1 | async-start | bytes 983040 | tf_op jit(solution)/shard_map/all_to_all | solution.py:416
  62.6 1.2 collective-permute-start.1
  63.8 2.0 %copy-start.3 = (bf16[224,64,128]{2,1,0:T(8,128)(2,1)S(1)}, bf16[224,64,128]{2,1,0:T(8,128)(2,1)}, u32[]{:S(2)}) copy-start(bf16[224,64,128]{2,1,0:T(8,128)(2,1)} %shard_map.69.bases_ref) | copy-start | bytes 11010052
  68.2 0.6 copy-start.8
  68.8 17.1 %all-to-all-start.2 = ((bf16[8,224,128]{2,1,0:T(8,128)(2,1)}), bf16[8,224,128]{2,1,0:T(8,128)(2,1)S(1)}, u32[]{:S(2)}, u32[]{:S(2)}) async-start(bf16[8,224,128]{2,1,0:T(8,128)(2,1)} %get-tuple-element.24), calls=%async_computation.2 | async-start | bytes 917504 | tf_op jit(solution)/shard_map/all_to_all | solution.py:416
  72.5 2.0 %copy-start.1 = (bf16[1,1024,1792]{2,1,0:T(8,128)(2,1)S(1)}, bf16[1,1024,1792]{2,1,0:T(8,128)(2,1)}, u32[]{:S(2)}) copy-start(bf16[1,1024,1792]{2,1,0:T(8,128)(2,1)} %param.4) | copy-start | bytes 11010052
  76.0 2.0 %collective-permute-start = (f32[1024,128]{1,0:T(8,128)S(1)}, f32[1024,128]{1,0:T(8,128)S(1)}, u32[]{:S(2)}, u32[]{:S(2)}) collective-permute-start(f32[1024,128]{1,0:T(8,128)S(1)} %shard_map.70.mine_ref.mine_old_ref), channel_id=1, source_target_pairs={{0,1},{1,0},{2,3},{3,2},{4,5},{5,4},{6,7},{7,6},{8,9},{9,8},{10,11... | collective-permute-start | bytes 1572872 | tf_op jit(solution)/shard_map/ppermute | solution.py:412
  87.1 16.9 %all-to-all-start.3 = ((bf16[8,224,128]{2,1,0:T(8,128)(2,1)}), bf16[8,224,128]{2,1,0:T(8,128)(2,1)S(1)}, u32[]{:S(2)}, u32[]{:S(2)}) async-start(bf16[8,224,128]{2,1,0:T(8,128)(2,1)} %bitcast.6), calls=%async_computation.3 | async-start | bytes 917504 | tf_op jit(solution)/shard_map/all_to_all | solution.py:416
  90.8 2.0 %copy-start.2 = (bf16[1,1024,1792]{2,1,0:T(8,128)(2,1)S(1)}, bf16[1,1024,1792]{2,1,0:T(8,128)(2,1)}, u32[]{:S(2)}) copy-start(bf16[1,1024,1792]{2,1,0:T(8,128)(2,1)} %param.4) | copy-start | bytes 11010052
  94.4 7.5 %collective-permute-start.2 = (f32[1024,128]{1,0:T(8,128)S(1)}, f32[1024,128]{1,0:T(8,128)S(1)}, u32[]{:S(2)}, u32[]{:S(2)}) collective-permute-start(f32[1024,128]{1,0:T(8,128)S(1)} %shard_map.74.mine_ref), channel_id=1, source_target_pairs={{0,1},{1,0},{2,3},{3,2},{4,5},{5,4},{6,7},{7,6},{8,9},{9,8},{10,11... | collective-permute-start | bytes 1572872 | tf_op jit(solution)/shard_map/ppermute | solution.py:412
  94.4 7.5 %copy-start.6 = (f32[1,512,128]{2,1,0:T(8,128)S(1)}, f32[1,512,128]{2,1,0:T(8,128)}, u32[]{:S(2)}) copy-start(f32[1,512,128]{2,1,0:T(8,128)} %param.5) | copy-start | bytes 786436
  104.0 2.0 %copy-start.4 = (bf16[224,64,128]{2,1,0:T(8,128)(2,1)S(1)}, bf16[224,64,128]{2,1,0:T(8,128)(2,1)}, u32[]{:S(2)}) copy-start(bf16[224,64,128]{2,1,0:T(8,128)(2,1)} %shard_map.69.bases_ref) | copy-start | bytes 11010052
  106.1 7.3 %copy-start.5 = (bf16[8,224,128]{2,1,0:T(8,128)(2,1)}, bf16[8,224,128]{2,1,0:T(8,128)(2,1)S(1)}, u32[]{:S(2)}) copy-start(bf16[8,224,128]{2,1,0:T(8,128)(2,1)S(1)} %all-to-all-done.3.blocks_ref) | copy-start | bytes 1376260
  108.3 15.0 %all-to-all-start.4 = ((f32[16,8,128]{2,1,0:T(8,128)}), f32[16,8,128]{2,1,0:T(8,128)S(1)}, u32[]{:S(2)}, u32[]{:S(2)}) async-start(f32[16,8,128]{2,1,0:T(8,128)} %shard_map.79), calls=%async_computation.4 | async-start | bytes 131072 | tf_op jit(solution)/shard_map/all_to_all | solution.py:525
  113.3 10.0 %copy-start.10 = (f32[1,64]{1,0:T(1,128)S(1)}, f32[1,64]{1,0:T(1,128)}, u32[]{:S(2)}) copy-start(f32[1,64]{1,0:T(1,128)} %mixing_ref.3) | copy-start | bytes 772

commit v4 on v3

--- a/solution.py
+++ b/solution.py
@@ -392,7 +392,8 @@
         values = jnp.concatenate(pair_of(bases, pair), axis=1)
         top = (RATE * FIRST_OLD / old_scale) * old + (RATE * FIRST_NEW / new_scale) * new
         square = old * old + new * new
-        put_pair(bases, pair, values - ratio(top, square * lax.rsqrt(square + TINY) + EPSILON_BASES))
+        bottom = square * lax.rsqrt(square + TINY) + EPSILON_BASES
+        put_pair(bases, pair, values - top * pltpu.reciprocal(bottom, approx=True))
         copy_of(bases, out_ref, out_sems, pair).start()
 
     each_pair(bases.shape[0], step)

time: 125 us -> 124 us (level)
  transfers between devices with their start and end apart: 7 -> 7, of which waited for: 5 -> 5; matrix products, arithmetic and copies ran while one was open for 0% -> 0% of each run, Pallas kernels for 24% -> 23%
where the time goes in v4:
time: 124 us; the launch traced here: 123 us
  Pallas kernels  45.1 us (36%)
  blocking collectives  32.6 us (26%)
  waiting for transfers between devices  17.3 us (14%)
  starting transfers between devices  16 us (13%)
  local copies, waits for them, and re-layouts  11.5 us (9%)
    pallas_call x14, Pallas kernels, call(): pl.pallas_call(kernel, out_shape=out_shape, grid=grid, in_specs=[whole] *...  45.1 us
    all_to_all x1, blocking collectives, exchange(): lax.all_to_all(array, 'expert', split_axis=0, concat_axis=0, tiled=True)  30.1 us
    all_to_all x3, waiting for transfers between devices, exchange(): lax.all_to_all(array, 'expert', split_axis=0, concat_axis=0, tiled=True)  14.2 us
    unnamed x22, local copies, waits for them, and re-layouts  11.5 us
    all_to_all x3, starting transfers between devices, exchange(): lax.all_to_all(array, 'expert', split_axis=0, concat_axis=0, tiled=True)  10.8 us
    all_to_all x1, starting transfers between devices, kernel_body(): lax.all_to_all(partial_two, ('expert', 'row'), split_axis=0, concat_axis=...  5.01 us
    ppermute x3, waiting for transfers between devices, swap_rows(): return lax.ppermute(array, 'row', [(0, 1), (1, 0)])  3.05 us
  transfers between devices with their start and end apart: 7, of which 5 were waited for; matrix products, arithmetic and copies ran while one was open for 0% of the time, Pallas kernels for 23%

profile of v4, /device:TPU:0, one launch (start us, length us, event | category | flops | bytes accessed | tf_op | source)
XLA Modules:
  0.0 123.2 jit_solution(2049253683326951434)
XLA Ops:
  0.6 2.5 %all-gather = f32[1,1024,128]{2,1,0:T(8,128)S(1)} all-gather(f32[1,512,128]{2,1,0:T(8,128)} %param.5), channel_id=2, replica_groups=mesh['layer'=2,'expert'=8,'row'=2] {'row'}, dimensions={1}, use_global_device_ids=true | all-gather | bytes 786432 | tf_op jit(solution)/shard_map/all_gather | solution.py:469
  3.1 0.0 copy-start
  3.1 2.0 %copy-done = bf16[1,1024,1792]{2,1,0:T(8,128)(2,1)S(1)} copy-done((bf16[1,1024,1792]{2,1,0:T(8,128)(2,1)S(1)}, bf16[1,1024,1792]{2,1,0:T(8,128)(2,1)}, u32[]{:S(2)}) %copy-start) | copy-done | bytes 3670040
  5.1 0.0 copy-start.9
  5.1 0.7 copy-done.9
  5.8 0.8 shard_map.67
  6.6 30.1 %all_to_all.25.sent_ref = bf16[8,432,128]{2,1,0:T(8,128)(2,1)} all-to-all(bf16[8,432,128]{2,1,0:T(8,128)(2,1)S(1)} %get-tuple-element.17), channel_id=1, replica_groups=mesh['layer'=2,'expert'=8,'row'=2] {'expert'}, dimensions={0} | all-to-all | bytes 1769472 | tf_op jit(solution)/shard_map/all_to_all | solution.py:417
  36.7 9.0 %shard_map.68 = (bf16[8,240,128]{2,1,0:T(8,128)(2,1)}, bf16[8,224,128]{2,1,0:T(8,128)(2,1)}, f32[8,64]{1,0:T(8,128)}) custom-call(bf16[8,432,128]{2,1,0:T(8,128)(2,1)} %all_to_all.25.sent_ref, f32[224,64,128]{2,1,0:T(8,128)} %bases_ref.5), custom_call_target="tpu_custom_call" | custom-call | flops 1409286144 | bytes 7340032 | tf_op jit(solution)/shard_map/pallas_call | solution.py:124
  45.7 0.0 copy-start.7
  45.7 3.5 %all-to-all-start.1 = ((bf16[8,240,128]{2,1,0:T(8,128)(2,1)}), bf16[8,240,128]{2,1,0:T(8,128)(2,1)S(1)}, u32[]{:S(2)}, u32[]{:S(2)}) async-start(bf16[8,240,128]{2,1,0:T(8,128)(2,1)} %get-tuple-element.18), calls=%async_computation.1 | async-start | bytes 983040 | tf_op jit(solution)/shard_map/all_to_all | solution.py:417
  49.2 7.3 %shard_map.69.bases_ref = bf16[224,64,128]{2,1,0:T(8,128)(2,1)} custom-call(f32[8,64]{1,0:T(8,128)} %get-tuple-element.19.mixing_ref.old_ref, f32[224,64,128]{2,1,0:T(8,128)} %bases_ref.5, bf16[8,224,128]{2,1,0:T(8,128)(2,1)} %get-tuple-element.20.blocks_ref.old_blocks_ref), custom_call_target="tpu_custom_call" | custom-call | flops 939524096 | bytes 14680064 | tf_op jit(solution)/shard_map/pallas_call | solution.py:124
  56.5 6.1 %all-to-all-done.1.panels_ref.sent_ref = bf16[8,240,128]{2,1,0:T(8,128)(2,1)S(1)} async-done(((bf16[8,240,128]{2,1,0:T(8,128)(2,1)}), bf16[8,240,128]{2,1,0:T(8,128)(2,1)S(1)}, u32[]{:S(2)}, u32[]{:S(2)}) %all-to-all-start.1) | async-done | bytes 491552 | tf_op jit(solution)/shard_map/all_to_all | solution.py:417
  62.6 0.1 collective-permute-start.1
  62.7 1.2 collective-permute-done.1.other_ref
  63.8 0.0 copy-done.7
  63.8 0.0 copy-start.3
  63.8 2.0 %copy-done.3 = bf16[224,64,128]{2,1,0:T(8,128)(2,1)S(1)} copy-done((bf16[224,64,128]{2,1,0:T(8,128)(2,1)S(1)}, bf16[224,64,128]{2,1,0:T(8,128)(2,1)}, u32[]{:S(2)}) %copy-start.3) | copy-done | bytes 3670040
  65.9 2.4 %shard_map.73 = (bf16[8,224,128]{2,1,0:T(8,128)(2,1)}, f32[8,64]{1,0:T(8,128)S(1)}, f32[8,64]{1,0:T(8,128)S(1)}) custom-call(f32[8,128]{1,0:T(8,128)S(1)} %shard_map.72.mine_ref, f32[8,128]{1,0:T(8,128)S(1)} %collective-permute-done.1.other_ref, f32[8,64]{1,0:T(8,128)S(1)} %copy-done.7, bf16[224,64,128]{2,1,0:T(8,128)(2,1)S(1)} %copy-done.3), custom_call_target="tpu_custom_call" | custom-call | flops 939524096 | bytes 3670016 | tf_op jit(solution)/shard_map/pallas_call | solution.py:124
  68.2 0.0 copy-start.8
  68.2 0.6 copy-done.8
  68.8 3.6 %all-to-all-start.2 = ((bf16[8,224,128]{2,1,0:T(8,128)(2,1)}), bf16[8,224,128]{2,1,0:T(8,128)(2,1)S(1)}, u32[]{:S(2)}, u32[]{:S(2)}) async-start(bf16[8,224,128]{2,1,0:T(8,128)(2,1)} %get-tuple-element.24), calls=%async_computation.2 | async-start | bytes 917504 | tf_op jit(solution)/shard_map/all_to_all | solution.py:417
  72.5 0.0 copy-start.1
  72.5 2.0 %copy-done.1 = bf16[1,1024,1792]{2,1,0:T(8,128)(2,1)S(1)} copy-done((bf16[1,1024,1792]{2,1,0:T(8,128)(2,1)S(1)}, bf16[1,1024,1792]{2,1,0:T(8,128)(2,1)}, u32[]{:S(2)}) %copy-start.1) | copy-done | bytes 3670040
  74.5 1.5 %shard_map.70.mine_ref.mine_old_ref = f32[1024,128]{1,0:T(8,128)S(1)} custom-call(bf16[1024,1792]{1,0:T(8,128)(2,1)S(1)} %bitcast.9, bf16[1024,128]{1,0:T(8,128)(2,1)S(1)} %get-tuple-element.16.low_ref, bf16[8,240,128]{2,1,0:T(8,128)(2,1)S(1)} %all-to-all-done.1.panels_ref.sent_ref), custom_call_target="tpu_custom_call" | custom-call | flops 469762048 | bytes 4128768 | tf_op jit(solution)/shard_map/pallas_call | solution.py:124
  76.0 0.1 collective-permute-start
  76.1 1.9 %collective-permute-done.other_ref.other_old_ref = f32[1024,128]{1,0:T(8,128)S(1)} collective-permute-done((f32[1024,128]{1,0:T(8,128)S(1)}, f32[1024,128]{1,0:T(8,128)S(1)}, u32[]{:S(2)}, u32[]{:S(2)}) %collective-permute-start) | collective-permute-done | bytes 524320 | tf_op jit(solution)/shard_map/ppermute | solution.py:413
  78.0 0.9 shard_map.71
  78.9 7.0 %all-to-all-done.2.panels_ref = bf16[8,224,128]{2,1,0:T(8,128)(2,1)S(1)} async-done(((bf16[8,224,128]{2,1,0:T(8,128)(2,1)}), bf16[8,224,128]{2,1,0:T(8,128)(2,1)S(1)}, u32[]{:S(2)}, u32[]{:S(2)}) %all-to-all-start.2) | async-done | bytes 458784 | tf_op jit(solution)/shard_map/all_to_all | solution.py:417
  85.9 1.2 shard_map.77
  87.1 3.7 %all-to-all-start.3 = ((bf16[8,224,128]{2,1,0:T(8,128)(2,1)}), bf16[8,224,128]{2,1,0:T(8,128)(2,1)S(1)}, u32[]{:S(2)}, u32[]{:S(2)}) async-start(bf16[8,224,128]{2,1,0:T(8,128)(2,1)} %bitcast.6), calls=%async_computation.3 | async-start | bytes 917504 | tf_op jit(solution)/shard_map/all_to_all | solution.py:417
  90.8 0.0 copy-start.2
  90.8 2.0 %copy-done.2 = bf16[1,1024,1792]{2,1,0:T(8,128)(2,1)S(1)} copy-done((bf16[1,1024,1792]{2,1,0:T(8,128)(2,1)S(1)}, bf16[1,1024,1792]{2,1,0:T(8,128)(2,1)}, u32[]{:S(2)}) %copy-start.2) | copy-done | bytes 3670040
  92.8 1.5 %shard_map.74.mine_ref = f32[1024,128]{1,0:T(8,128)S(1)} custom-call(bf16[1024,1792]{1,0:T(8,128)(2,1)S(1)} %bitcast.11, bf16[1024,128]{1,0:T(8,128)(2,1)S(1)} %get-tuple-element.22.low_ref, bf16[8,224,128]{2,1,0:T(8,128)(2,1)S(1)} %all-to-all-done.2.panels_ref), custom_call_target="tpu_custom_call" | custom-call | flops 469762048 | bytes 4128768 | tf_op jit(solution)/shard_map/pallas_call | solution.py:124
  94.4 0.1 collective-permute-start.2
  94.4 0.0 copy-start.6
  94.5 7.4 %shard_map.76.bases_ref = f32[224,64,128]{2,1,0:T(8,128)} custom-call(f32[8,64]{1,0:T(8,128)} %get-tuple-element.19.mixing_ref.old_ref, f32[224,64,128]{2,1,0:T(8,128)} %bases_ref.5, bf16[8,224,128]{2,1,0:T(8,128)(2,1)} %get-tuple-element.20.blocks_ref.old_blocks_ref), custom_call_target="tpu_custom_call" | custom-call | flops 939524096 | bytes 14680064 | tf_op jit(solution)/shard_map/pallas_call | solution.py:124
  101.9 0.0 collective-permute-done.2.other_ref
  101.9 0.0 copy-done.6
  101.9 1.0 shard_map.75
  102.9 1.1 all-to-all-done.3.blocks_ref
  104.0 0.0 copy-start.4
  104.0 2.0 %copy-done.4 = bf16[224,64,128]{2,1,0:T(8,128)(2,1)S(1)} copy-done((bf16[224,64,128]{2,1,0:T(8,128)(2,1)S(1)}, bf16[224,64,128]{2,1,0:T(8,128)(2,1)}, u32[]{:S(2)}) %copy-start.4) | copy-done | bytes 3670040
  106.1 0.0 copy-start.5
  106.1 2.3 %shard_map.79 = f32[16,8,128]{2,1,0:T(8,128)} custom-call(bf16[224,64,128]{2,1,0:T(8,128)(2,1)S(1)} %copy-done.4, bf16[8,224,128]{2,1,0:T(8,128)(2,1)S(1)} %all-to-all-done.3.blocks_ref), custom_call_target="tpu_custom_call" | custom-call | flops 469762048 | bytes 3670016 | tf_op jit(solution)/shard_map/pallas_call | solution.py:124
  108.3 5.0 %all-to-all-start.4 = ((f32[16,8,128]{2,1,0:T(8,128)}), f32[16,8,128]{2,1,0:T(8,128)S(1)}, u32[]{:S(2)}, u32[]{:S(2)}) async-start(f32[16,8,128]{2,1,0:T(8,128)} %shard_map.79), calls=%async_computation.4 | async-start | bytes 131072 | tf_op jit(solution)/shard_map/all_to_all | solution.py:526
  113.3 0.0 copy-done.5
  113.3 0.0 copy-start.10
  113.3 9.3 %shard_map.78 = f32[224,64,128]{2,1,0:T(8,128)} custom-call(f32[8,64]{1,0:T(8,128)} %get-tuple-element.19.mixing_ref.old_ref, f32[8,64]{1,0:T(8,128)} %copy-done.8, f32[224,64,128]{2,1,0:T(8,128)} %shard_map.76.bases_ref, bf16[8,224,128]{2,1,0:T(8,128)(2,1)} %get-tuple-element.20.blocks_ref.old_blocks_ref, bf16[8,224,128]{2,1,0:T(8,128)(2,1)} %copy-done.5), custom_call_target="tpu_custom_call" | custom-call | flops 1879048192 | bytes 14680064 | tf_op jit(solution)/shard_map/pallas_call | solution.py:124
  122.6 0.0 all-to-all-done.4.sums_ref
  122.6 0.0 copy-done.10
  122.6 0.6 shard_map.80
  (1 shorter events, 0.0 us)
Async XLA Ops:
  3.1 2.0 %copy-start = (bf16[1,1024,1792]{2,1,0:T(8,128)(2,1)S(1)}, bf16[1,1024,1792]{2,1,0:T(8,128)(2,1)}, u32[]{:S(2)}) copy-start(bf16[1,1024,1792]{2,1,0:T(8,128)(2,1)} %param.4) | copy-start | bytes 11010052
  5.1 0.7 copy-start.9
  45.7 18.1 %copy-start.7 = (f32[8,64]{1,0:T(8,128)S(1)}, f32[8,64]{1,0:T(8,128)}, u32[]{:S(2)}) copy-start(f32[8,64]{1,0:T(8,128)} %get-tuple-element.19.mixing_ref.old_ref) | copy-start | bytes 6148
  45.7 16.9 %all-to-all-start.1 = ((bf16[8,240,128]{2,1,0:T(8,128)(2,1)}), bf16[8,240,128]{2,1,0:T(8,128)(2,1)S(1)}, u32[]{:S(2)}, u32[]{:S(2)}) async-start(bf16[8,240,128]{2,1,0:T(8,128)(2,1)} %get-tuple-element.18), calls=%async_computation.1 | async-start | bytes 983040 | tf_op jit(solution)/shard_map/all_to_all | solution.py:417
  62.6 1.2 collective-permute-start.1
  63.8 2.0 %copy-start.3 = (bf16[224,64,128]{2,1,0:T(8,128)(2,1)S(1)}, bf16[224,64,128]{2,1,0:T(8,128)(2,1)}, u32[]{:S(2)}) copy-start(bf16[224,64,128]{2,1,0:T(8,128)(2,1)} %shard_map.69.bases_ref) | copy-start | bytes 11010052
  68.2 0.6 copy-start.8
  68.8 17.1 %all-to-all-start.2 = ((bf16[8,224,128]{2,1,0:T(8,128)(2,1)}), bf16[8,224,128]{2,1,0:T(8,128)(2,1)S(1)}, u32[]{:S(2)}, u32[]{:S(2)}) async-start(bf16[8,224,128]{2,1,0:T(8,128)(2,1)} %get-tuple-element.24), calls=%async_computation.2 | async-start | bytes 917504 | tf_op jit(solution)/shard_map/all_to_all | solution.py:417
  72.5 2.0 %copy-start.1 = (bf16[1,1024,1792]{2,1,0:T(8,128)(2,1)S(1)}, bf16[1,1024,1792]{2,1,0:T(8,128)(2,1)}, u32[]{:S(2)}) copy-start(bf16[1,1024,1792]{2,1,0:T(8,128)(2,1)} %param.4) | copy-start | bytes 11010052
  76.0 2.0 %collective-permute-start = (f32[1024,128]{1,0:T(8,128)S(1)}, f32[1024,128]{1,0:T(8,128)S(1)}, u32[]{:S(2)}, u32[]{:S(2)}) collective-permute-start(f32[1024,128]{1,0:T(8,128)S(1)} %shard_map.70.mine_ref.mine_old_ref), channel_id=1, source_target_pairs={{0,1},{1,0},{2,3},{3,2},{4,5},{5,4},{6,7},{7,6},{8,9},{9,8},{10,11... | collective-permute-start | bytes 1572872 | tf_op jit(solution)/shard_map/ppermute | solution.py:413
  87.1 16.9 %all-to-all-start.3 = ((bf16[8,224,128]{2,1,0:T(8,128)(2,1)}), bf16[8,224,128]{2,1,0:T(8,128)(2,1)S(1)}, u32[]{:S(2)}, u32[]{:S(2)}) async-start(bf16[8,224,128]{2,1,0:T(8,128)(2,1)} %bitcast.6), calls=%async_computation.3 | async-start | bytes 917504 | tf_op jit(solution)/shard_map/all_to_all | solution.py:417
  90.8 2.0 %copy-start.2 = (bf16[1,1024,1792]{2,1,0:T(8,128)(2,1)S(1)}, bf16[1,1024,1792]{2,1,0:T(8,128)(2,1)}, u32[]{:S(2)}) copy-start(bf16[1,1024,1792]{2,1,0:T(8,128)(2,1)} %param.4) | copy-start | bytes 11010052
  94.4 7.5 %collective-permute-start.2 = (f32[1024,128]{1,0:T(8,128)S(1)}, f32[1024,128]{1,0:T(8,128)S(1)}, u32[]{:S(2)}, u32[]{:S(2)}) collective-permute-start(f32[1024,128]{1,0:T(8,128)S(1)} %shard_map.74.mine_ref), channel_id=1, source_target_pairs={{0,1},{1,0},{2,3},{3,2},{4,5},{5,4},{6,7},{7,6},{8,9},{9,8},{10,11... | collective-permute-start | bytes 1572872 | tf_op jit(solution)/shard_map/ppermute | solution.py:413
  94.4 7.5 %copy-start.6 = (f32[1,512,128]{2,1,0:T(8,128)S(1)}, f32[1,512,128]{2,1,0:T(8,128)}, u32[]{:S(2)}) copy-start(f32[1,512,128]{2,1,0:T(8,128)} %param.5) | copy-start | bytes 786436
  104.0 2.0 %copy-start.4 = (bf16[224,64,128]{2,1,0:T(8,128)(2,1)S(1)}, bf16[224,64,128]{2,1,0:T(8,128)(2,1)}, u32[]{:S(2)}) copy-start(bf16[224,64,128]{2,1,0:T(8,128)(2,1)} %shard_map.69.bases_ref) | copy-start | bytes 11010052
  106.1 7.3 %copy-start.5 = (bf16[8,224,128]{2,1,0:T(8,128)(2,1)}, bf16[8,224,128]{2,1,0:T(8,128)(2,1)S(1)}, u32[]{:S(2)}) copy-start(bf16[8,224,128]{2,1,0:T(8,128)(2,1)S(1)} %all-to-all-done.3.blocks_ref) | copy-start | bytes 1376260
  108.3 14.3 %all-to-all-start.4 = ((f32[16,8,128]{2,1,0:T(8,128)}), f32[16,8,128]{2,1,0:T(8,128)S(1)}, u32[]{:S(2)}, u32[]{:S(2)}) async-start(f32[16,8,128]{2,1,0:T(8,128)} %shard_map.79), calls=%async_computation.4 | async-start | bytes 131072 | tf_op jit(solution)/shard_map/all_to_all | solution.py:526
  113.3 9.3 %copy-start.10 = (f32[1,64]{1,0:T(1,128)S(1)}, f32[1,64]{1,0:T(1,128)}, u32[]{:S(2)}) copy-start(f32[1,64]{1,0:T(1,128)} %mixing_ref.3) | copy-start | bytes 772
